TPU v7x, 32 devices: a whole 2x2x4 slice. The times are simulated.
32 devices in a mesh: dp: 16 (over z, x, core), fsdp: 2 (over y).
Axes of the slice: x: 2, y: 2, z: 4, core: 2. Of those that a mesh axis runs over, the one named last changes fastest.
Arguments:
- alignment_input: bfloat16 [32, 32, 32, 768], P(('dp', 'fsdp')), may hold values from -6 to 6
- sequence_mask: int32 [32, 32], P(('dp', 'fsdp')), may hold values from 0 to 1, as said below
- column_length: int32 [32], P(('dp', 'fsdp')), may hold values from 8 to 32, as said below
- output_cotangent: bfloat16 [32, 32, 32, 768], P(('dp', 'fsdp')), may hold values from -6 to 6
- row_projection_weight: bfloat16 [768, 2304], P('fsdp', 'dp'), may hold values from -0.21875 to 0.21875
- row_out_weight: bfloat16 [768, 768], P('dp', 'fsdp'), may hold values from -1.25 to 1.25
- column_projection_weight: bfloat16 [768, 2304], P('fsdp', 'dp'), may hold values from -0.21875 to 0.21875
- column_out_weight: bfloat16 [768, 768], P('dp', 'fsdp'), may hold values from -1.25 to 1.25
- feedforward_in_weight: bfloat16 [768, 3072], P('fsdp', 'dp'), may hold values from -0.21875 to 0.21875
- feedforward_out_weight: bfloat16 [3072, 768], P('dp', 'fsdp'), may hold values from -0.109375 to 0.109375
- layer_norm_gain: bfloat16 [3, 768], P(None, ('dp', 'fsdp')), may hold values from 0.5 to 1.5
- layer_norm_bias: bfloat16 [3, 768], P(None, ('dp', 'fsdp')), may hold values from -2.5 to 2.5
Outputs:
- layer_out: bfloat16 [32, 32, 32, 768], P(('dp', 'fsdp'))
- grad_input: float32 [32, 32, 32, 768], P(('dp', 'fsdp'))
- grad_row_qkv: float32 [768, 2304], P('fsdp', 'dp')
- grad_row_out: float32 [768, 768], P('dp', 'fsdp')
- grad_col_qkv: float32 [768, 2304], P('fsdp', 'dp')
- grad_col_out: float32 [768, 768], P('dp', 'fsdp')
- grad_ffn_in: float32 [768, 3072], P('fsdp', 'dp')
- grad_ffn_out: float32 [3072, 768], P('dp', 'fsdp')
- grad_norm_gain: float32 [3, 768], P(None, ('dp', 'fsdp'))
- grad_norm_bias: float32 [2, 768], P(None, ('dp', 'fsdp'))
- grad_ffn_norm_bias: float32 [768], P(('dp', 'fsdp'))
- penalty: float32 [], replicated
Inputs may be any that keep to these rules, and one draw needn't show every extreme that they name: `sequence_mask`: an alignment's true sequences are its first rows; each alignment has 8 or more, and alignment 0 has all 32. `column_length`: the true columns of alignment a rise with a, from 8 at alignment 0 to 32 at the last alignment, within one of the straight line between them.
All inputs are finite; a program needn't handle non-finite values.
Results may differ from a plain program's by a relative error of at most 0.024.
Values may be sent and summed in bfloat16 or wider, within the bound.
No kernel may reach another device: no remote copies, remote signals or barrier semaphores. Data moves between devices by JAX's collectives and lax.ppermute only.
A program may use at most 192 MiB of HBM per device.

v0:
```python
import jax
import jax.numpy as jnp
import numpy as np
from jax import lax
from jax.experimental import pallas as pl
from jax.experimental.pallas import tpu as pltpu
from jax.sharding import PartitionSpec as P

HD = 64
AXES = ("dp", "fsdp")
norm_eps = 1e-05
penalty_weight = 1.0
masked_score = -1000000000.0
never = -1e30

F32 = jnp.float32
BF16 = jnp.bfloat16
MIB = 1 << 20
PITCH = 33


def dot(a, b, ca, cb):
    return lax.dot_general(a, b, (((ca,), (cb,)), ((), ())), preferred_element_type=F32)


class Weights:
    def __init__(self, bufs, row0, rows, whole_rows, width, blocked, table=0):
        self.raw = self.here = False
        self.dtype = BF16
        self.bufs, self.row0, self.rows, self.table = bufs, row0, rows, table
        self.whole_rows, self.width, self.blocked = whole_rows, width, blocked


    @staticmethod
    def of(a):
        w = Weights([a], 0, a.shape[0], a.shape[0], a.shape[1], False)
        w.dtype = a.dtype
        return w

    @staticmethod
    def held(a):
        w = Weights.of(a)
        w.here = True
        return w

    def copies(self, plan):
        if self.here:
            return 0
        return sum(b.shape[0] for b in self.bufs) if self.blocked else 1


class Loaded:
    def __init__(self, ref, copies):
        self.ref, self.copies = ref, copies

    def start(self, part=None):
        for c in self.copies if part is None else self.copies[part : part + 1]:
            c.start()

    def wait(self):
        for c in self.copies:
            c.wait()
        return self.ref


class Out:
    def __init__(self, shape, dtype, vmem=True, hbm=False):
        self.shape, self.dtype, self.vmem, self.hbm = shape, dtype, vmem, hbm
        self.parts = max(1, shape[1] // 768) if hbm else 0


def fused(
    name, body, smem, ins, weights, outs, grads, plan, resident, micros, scratch=(), deps=(), fetch=()
):
    arrays, index, spaces = [], {}, []

    def slot(a):
        if id(a) not in index:
            index[id(a)] = len(arrays)
            stays = id(a) in resident
            spaces.append(pltpu.VMEM if stays else pltpu.HBM)
            arrays.append(pltpu.with_memory_space_constraint(a, spaces[-1]))
        return index[id(a)]

    in_slots = [slot(a) for a in ins]
    w_slots = [[slot(b) for b in w.bufs] for w in (*weights, *fetch)]
    weights = list(weights)
    n_weights = len(weights)
    for a in deps:
        arrays.append(a)
        spaces.append(pl.ANY)
    n_smem = len(smem)
    vm, n_sem = [], 0
    for a in ins:
        if id(a) not in resident:
            vm.append(pltpu.VMEM(a.shape, a.dtype))
            n_sem += 1
    for w in (*weights, *fetch):
        n_sem += w.copies(plan)
    for w in weights:
        if w.here:
            continue
        raw = (w.whole_rows // w.rows * plan.fsdp, w.rows, w.width // plan.fsdp)
        vm.append(pltpu.VMEM(raw if w.raw else (w.whole_rows, w.width), BF16))
    out_shapes, out_spaces = [], []
    for o in outs:
        if o.vmem:
            out_shapes.append(pltpu.VMEM(o.shape, o.dtype))
            out_spaces.append(pltpu.VMEM)
        else:
            vm.append(pltpu.VMEM(o.shape, o.dtype))
        if o.hbm:
            out_shapes.append(pltpu.HBM(o.shape, o.dtype))
            out_spaces.append(pltpu.HBM)
            n_sem += o.parts
    f_at = len(out_shapes)
    for w in fetch:
        out_shapes.append(pltpu.VMEM((w.whole_rows, w.width), w.dtype))
        out_spaces.append(pltpu.VMEM)
    g_at = len(out_shapes)
    width = plan.width
    for rows in grads:
        vm.append(pltpu.VMEM((rows, width), BF16))
        n_sem += plan.dp * plan.fsdp if plan.fast else 1
    if grads and plan.fast:
        per = sum(rows // plan.dp for rows in grads)
        shape = pltpu.HBM((plan.slots, per, width // plan.fsdp), BF16)
        out_shapes += [shape, shape]
    elif grads:
        out_shapes += [pltpu.HBM((rows, width), BF16) for rows in grads]
    out_spaces += [pltpu.HBM] * (len(out_shapes) - g_at)
    n_in, n_out, n_vm = len(arrays), len(out_shapes), len(vm)
    used_vmem = sum(int(np.prod(m.shape)) * np.dtype(m.dtype).itemsize for m in (*vm, *scratch))

    def kernel(*refs):
        sm = refs[:n_smem]
        hb = refs[n_smem : n_smem + n_in]
        ob = refs[n_smem + n_in : n_smem + n_in + n_out]
        rest = refs[n_smem + n_in + n_out :]
        vrefs, extra, sems = list(rest[:n_vm]), rest[n_vm:-1], rest[-1]
        used = [0]

        def sem():
            used[0] += 1
            return sems.at[used[0] - 1]

        loads = Loads()
        for a, s in zip(ins, in_slots):
            if id(a) in resident:
                loads.append(Loaded(hb[s], []))
            else:
                ref = vrefs.pop(0)
                loads.append(Loaded(ref, [pltpu.make_async_copy(hb[s], ref, sem())]))
        wl = []
        for n, (w, slots) in enumerate(zip((*weights, *fetch), w_slots)):
            copies = []
            if w.here:
                dst = hb[slots[0]]
            elif n < n_weights:
                dst = vrefs.pop(0)
            else:
                dst = ob[f_at + n - n_weights]
            if w.here:
                pass
            elif w.blocked:
                cols = w.width // plan.fsdp
                count = 0
                for s in slots:
                    for j in range(arrays[s].shape[0]):
                        block = sm[w.table][count] if w.table is not None else count
                        count += 1
                        row = (block // plan.fsdp) * w.rows
                        col = (block % plan.fsdp) * cols
                        if w.table is not None:
                            row, col = pl.multiple_of(row, 16), pl.multiple_of(col, 128)
                        spot = dst.at[pl.ds(row, w.rows), pl.ds(col, cols)]
                        if w.raw:
                            spot = dst.at[count - 1]
                        src = hb[s].at[j, pl.ds(w.row0, w.rows), :]
                        copies.append(pltpu.make_async_copy(src, spot, sem()))
            else:
                copies.append(pltpu.make_async_copy(hb[slots[0]], dst, sem()))
            (wl if n < n_weights else loads.fetched).append(Loaded(dst, copies))
        ol = []
        at = 0
        for o in outs:
            if o.vmem:
                ref = ob[at]
                at += 1
            else:
                ref = vrefs.pop(0)
            copies = []
            if o.hbm:
                for k in range(o.parts):
                    lanes = slice(None)
                    if o.parts > 1:
                        lanes = pl.ds(k * 768, 768)
                    copies.append(
                        pltpu.make_async_copy(ref.at[:, lanes], ob[at].at[:, lanes], sem())
                    )
                at += 1
            ol.append(Loaded(ref, copies))
        gl = []
        row0 = 0
        for k, rows in enumerate(grads):
            src = vrefs.pop(0)
            if plan.fast:
                gl.append(Blocks(src, ob[g_at], ob[g_at + 1], sm[1], plan, rows, row0, sem))
                row0 += rows // plan.dp
            else:
                gl.append(Loaded(src, [pltpu.make_async_copy(src, ob[g_at + k], sem())]))
        for l in (*loads[:1], *wl[:1], *loads[1:], *wl[1:]):
            l.start()
        body(sm[:1] + sm[3:] if name == "rowf" else sm[3:], loads, wl, ol, gl, extra)
        for l in (*ol, *gl, *loads.fetched):
            l.wait()

    res = pl.pallas_call(
        kernel,
        name=name,
        out_shape=out_shapes,
        in_specs=[pl.BlockSpec(memory_space=pltpu.SMEM)] * n_smem
        + [pl.BlockSpec(memory_space=m) for m in spaces],
        out_specs=[pl.BlockSpec(memory_space=m) for m in out_spaces],
        scratch_shapes=vm + list(scratch) + [pltpu.SemaphoreType.DMA((n_sem,))],
        compiler_params=pltpu.CompilerParams(vmem_limit_bytes=used_vmem + 7 * MIB),
        cost_estimate=pl.CostEstimate(
            flops=int(micros * 1e6), bytes_accessed=int(micros * 3e3), transcendentals=0
        ),
    )(*smem, *arrays)
    got, at = [], 0
    for o in outs:
        both = res[at : at + o.vmem + o.hbm]
        at += o.vmem + o.hbm
        if o.vmem:
            resident[id(both[0])] = both[0]
        got.append(both[0] if len(both) == 1 else both)
    for a in res[f_at:g_at]:
        resident[id(a)] = a
        got.append(Weights.held(a))
    return got, res[g_at:]


class Loads(list):
    def __init__(self):
        self.fetched = []

    def later(self):
        for l in self.fetched:
            l.start()


class Blocks:
    def __init__(self, ref, kept, sent, table, plan, rows, row0, sem):
        self.ref, self.plan = ref, plan
        self.per, self.cols = rows // plan.dp, plan.width // plan.fsdp
        self.kept, self.sent, self.table, self.row0 = kept, sent, table, row0
        self.sems = [sem() for _ in range(plan.dp * plan.fsdp)]
        self.begun = 0

    def copy(self, n, out, slot):
        row, col = (n // self.plan.fsdp) * self.per, (n % self.plan.fsdp) * self.cols
        return pltpu.make_async_copy(
            self.ref.at[row : row + self.per, col : col + self.cols],
            out.at[slot, pl.ds(self.row0, self.per), :],
            self.sems[n],
        )

    def start(self, rows=None):
        rows = self.ref.shape[0] if rows is None else rows
        end = rows // self.per * self.plan.fsdp
        slots = self.plan.slots
        for n in range(self.begun, end):
            place = self.table[n]

            @pl.when(place < slots)
            def _():
                self.copy(n, self.kept, place).start()

            @pl.when(place >= slots)
            def _():
                self.copy(n, self.sent, place - slots).start()

        self.begun = end

    def wait(self):
        for n in range(self.begun):
            self.copy(n, self.kept, 0).wait()


def stamp(out):
    out.ref[...] = jnp.zeros(out.ref.shape, out.ref.dtype)
    out.start()


def normal_form(v):
    centred = v - jnp.mean(v, -1, keepdims=True)
    rstd = lax.rsqrt(jnp.mean(centred * centred, -1, keepdims=True) + norm_eps)
    return centred * rstd, rstd


def norm_rows(src, dst, gb, k, total):
    for t in range(0, total, 256):
        xhat, _ = normal_form(src[t : t + 256, :].astype(F32))
        dst[t : t + 256, :] = (xhat * gb[k : k + 1, :] + gb[k + 3 : k + 4, :]).astype(BF16)


def norm_back(dn_ref, src, base, gb, k, total, emit, sums):
    gain = gb[k : k + 1, :]
    gain_sum = jnp.zeros_like(gain)
    bias_sum = jnp.zeros_like(gain)
    for t in range(0, total, 256):
        xhat, rstd = normal_form(src[t : t + 256, :].astype(F32))
        dn = dn_ref[t : t + 256, :]
        gain_sum = gain_sum + jnp.sum(dn * xhat, 0, keepdims=True)
        bias_sum = bias_sum + jnp.sum(dn, 0, keepdims=True)
        dx = dn * gain
        low = jnp.mean(dx, -1, keepdims=True)
        mix = jnp.mean(dx * xhat, -1, keepdims=True)
        emit(t, base[t : t + 256, :].astype(F32) + rstd * (dx - low - xhat * mix))
    none = jnp.zeros((1, gain.shape[1]), F32)
    rows = [none] * (2 * k) + [gain_sum, bias_sum] + [none] * (6 - 2 * k)
    sums[...] = jnp.concatenate(rows, 0)


def head_masks(lanes):
    lane = lax.broadcasted_iota(jnp.int32, (1, lanes), 1)
    low = ((lane // HD) % 2 == 0).astype(F32)
    return low.astype(BF16), (1.0 - low).astype(BF16)


def four(ref, col):
    return jnp.concatenate([ref[g * 256 : (g + 1) * 256, col : col + 128] for g in range(4)], 1)


def pick(big):
    seg = lax.broadcasted_iota(jnp.int32, (32, 256), 1) // 32
    out = big[:32, :]
    for k in range(1, 8):
        out = jnp.where(seg == k, big[k * 32 : (k + 1) * 32, :], out)
    out = out[:, :128] + out[:, 128:]
    out = out + pltpu.roll(out, 64, 1)
    return out + pltpu.roll(out, 32, 1)


def spread(small):
    seg = lax.broadcasted_iota(jnp.int32, (32, 256), 1) // 32
    wide = jnp.concatenate([small, small], 1)
    return jnp.concatenate([jnp.where(seg == k, wide, 0.0).astype(BF16) for k in range(8)], 0)


def gathered_norms(blocks, table):
    slots = blocks.shape[0]
    values = jnp.sum(blocks[...].astype(F32), 1).astype(BF16)
    place = lax.broadcasted_iota(jnp.int32, (slots, 1), 0)
    owner = jnp.zeros((slots, 1), jnp.int32)
    for j in range(slots):
        owner = jnp.where(place == j, table[j], owner)
    share = 768 // slots
    lane = lax.broadcasted_iota(jnp.int32, (1, 768), 1)
    row = lax.broadcasted_iota(jnp.int32, (values.shape[1], 1), 0)
    mine = lane // share == owner
    rows = []
    for k in range(6):
        spot = (row == k * share + lane % share).astype(F32).astype(BF16)
        rows.append(jnp.sum(jnp.where(mine, dot(values, spot, 1, 0), 0.0), 0, keepdims=True))
    count = jnp.where(lax.broadcasted_iota(jnp.int32, (1, values.shape[1]), 1) == 6 * share, 1.0, 0.0)
    total = jnp.sum(values.astype(F32) * count)
    rows.append(jnp.full((1, 768), total, F32))
    rows.append(jnp.zeros((1, 768), F32))
    return jnp.concatenate(rows, 0)


def row_forward(sm, I, W, O, G, X):
    ints, flts = sm[-2:]
    x = I[0]
    normed, packed, mixed, prob, logp, ent, norms = O
    sc = X[0]
    if len(W) > 1:
        norms.ref[...] = gathered_norms(W[0].wait(), sm[0])
    else:
        norms.ref[...] = I[1].wait()[...]
    norms.start()
    xr, g = x.wait(), norms.ref
    norm_rows(xr, normed.ref, g, 0, 1024)
    normed.start()
    wt = W[-1].wait()
    nr = normed.ref[...]
    n_seq, n_col = ints[0], ints[1]
    keep = (lax.broadcasted_iota(jnp.int32, (1024, 1), 0) // 32 < n_seq).astype(F32)
    width = nr.shape[1]
    heads = width // HD
    pr = packed.ref
    for n in range(0, 3 * width, 256):
        out = dot(nr, wt[n : n + 256, :], 1, 1)
        if n < width:
            out = out * keep
        pr[:, n : n + 256] = out.astype(BF16)
        if (n + 256) % 768 == 0:
            packed.start(n // 768)
    halves = head_masks(512)
    for m in range(heads // 2):
        q, k = four(pr, m * 128), four(pr, width + m * 128)
        for e in range(2):
            h = 2 * m + e
            sc[h * 32 : (h + 1) * 32, :] = pick(dot(q * halves[e], k, 1, 1))
    lane = lax.broadcasted_iota(jnp.int32, (1, 128), 1) % 32
    s = jnp.where(lane < n_col, sc[...] * flts[0], masked_score)
    top = jnp.max(s, -1, keepdims=True)
    total = jnp.sum(jnp.exp(s - top), -1, keepdims=True) * 0.25
    lp = s - (top + jnp.log(total))
    p = jnp.exp(lp)
    prob.ref[...] = p
    logp.ref[...] = lp
    prob.start()
    logp.start()
    entropy = jnp.sum(p * lp, -1, keepdims=True) * -0.25
    row = lax.broadcasted_iota(jnp.int32, entropy.shape, 0) % 32
    total = jnp.sum(jnp.where(row < n_col, entropy, 0.0))
    share = total / norms.ref[6:7, :]
    ent.ref[...] = jnp.where(lax.broadcasted_iota(jnp.int32, ent.ref.shape, 0) == 6, share, 0.0)
    ent.start()
    second = (lax.broadcasted_iota(jnp.int32, (1, 512), 1) // HD) % 2 == 1
    for m in range(heads // 2):
        v = four(pr, 2 * width + m * 128)
        both = [
            dot(spread(prob.ref[h * 32 : (h + 1) * 32, :]), v, 1, 0) for h in (2 * m, 2 * m + 1)
        ]
        out = jnp.where(second, both[1], both[0]).astype(BF16)
        for t in range(4):
            mixed.ref[t * 256 : (t + 1) * 256, m * 128 : (m + 1) * 128] = out[
                :, t * 128 : (t + 1) * 128
            ]
    mixed.start()


def stacked(x, halves):
    return jnp.concatenate([x * halves[0], x * halves[1]], 0)


def segment(rows):
    return (lax.broadcasted_iota(jnp.int32, (rows, 256), 1) // 32) % 4


def pick_four(big):
    seg = segment(32)
    out = big[:32, :]
    for k in range(1, 4):
        out = jnp.where(seg == k, big[k * 32 : (k + 1) * 32, :], out)
    return out


def spread_four(small):
    seg = segment(32)
    return jnp.concatenate([jnp.where(seg == k, small, 0.0).astype(BF16) for k in range(4)], 0)


def unstack(both):
    lane = lax.broadcasted_iota(jnp.int32, (128, 128), 1)
    return jnp.where(lane < HD, both[:128], both[128:])


def to_columns(src, take):
    for t in range(0, 1024, 256):
        lanes = [
            jnp.concatenate([src[j, pl.ds(t // 32 + k, 32, stride=PITCH), :] for k in range(8)], 0)
            for j in range(src.shape[0])
        ]
        take(t, jnp.concatenate(lanes, 1))


def put(dst, start, n, value):
    for r in range(value.shape[0] // 32):
        at = (start // 32 + r) * PITCH
        for j in range(value.shape[1] // 128):
            piece = value[r * 32 : (r + 1) * 32, j * 128 : (j + 1) * 128]
            dst[n // 128 + j, at : at + 32, :] = piece


def column_forward(sm, I, W, O, G, X):
    x, mixed_row, gb = I
    after, normed, packed = O
    (ar,) = X
    width = normed.ref.shape[1]
    mr, xr = mixed_row.wait(), x.wait()
    wo = W[0].wait()
    for n in range(0, width, 256):
        out = xr[:, n : n + 256].astype(F32) + dot(mr[...], wo[:, n : n + 256], 1, 0)
        put(ar, 0, n, out)
    g = gb.wait()

    def take(t, rows):
        after.ref[t : t + 256, :] = rows

    to_columns(ar, take)
    after.start()
    norm_rows(after.ref, normed.ref, g, 1, 1024)
    normed.start()
    wt = W[1].wait()
    nr = normed.ref[...]
    pr = packed.ref
    for n in range(0, 3 * width, 256):
        pr[:, n : n + 256] = dot(nr, wt[n : n + 256, :], 1, 1).astype(BF16)
        if (n + 256) % 768 == 0:
            packed.start(n // 768)


def column_softmax(sc, n_seq):
    def block(b, carry):
        at = pl.ds(pl.multiple_of(b * 32, 32), 32)
        s = sc[at, :]
        s = jnp.where(lax.broadcasted_iota(jnp.int32, s.shape, 0) < n_seq, s, never)
        p = jnp.exp(s - jnp.max(s, 0, keepdims=True))
        sc[at, :] = p * (1.0 / jnp.sum(p, 0, keepdims=True))
        return carry

    lax.fori_loop(0, sc.shape[0] // 32, block, 0)


def column_attend(sm, I, W, O, G, X):
    (ints,) = sm
    (mixed,) = O
    (sc,) = X
    width = mixed.ref.shape[1]
    pr = I[0].wait()
    halves = head_masks(128)

    def scores(b, carry):
        rows = pl.ds(pl.multiple_of(b * 128, 128), 128)
        at = pl.ds(pl.multiple_of(b * 32, 32), 32)
        for lo in range(0, width, 128):
            qs = stacked(pr[rows, lo : lo + 128] * 0.125, halves)
            k = pr[rows, width + lo : width + lo + 128]
            sc[at, 2 * lo : 2 * lo + 256] = pick_four(dot(k, qs, 1, 1))
        return carry

    lax.fori_loop(0, 8, scores, 0)
    column_softmax(sc, ints[0])

    def mix(b, carry):
        rows = pl.ds(pl.multiple_of(b * 128, 128), 128)
        at = pl.ds(pl.multiple_of(b * 32, 32), 32)
        for lo in range(0, width, 128):
            v = pr[rows, 2 * width + lo : 2 * width + lo + 128]
            p = spread_four(sc[at, 2 * lo : 2 * lo + 256])
            mixed.ref[rows, lo : lo + 128] = unstack(dot(p, v, 0, 0)).astype(BF16)
        return carry

    lax.fori_loop(0, 8, mix, 0)
    mixed.start()


def column_all(sm, I, W, O, G, X):
    column_forward((), I, W, O[:3], G, X[:1])
    column_attend(sm, [Loaded(O[2].ref, [])], W, O[3:], G, X[1:])


def feed_forward(sm, I, W, O, G, X):
    after_row, mixed, gb = I
    after, normed, active, slope = O
    width = normed.ref.shape[1]
    hidden = active.ref.shape[1]
    ar, mr = after_row.wait(), mixed.wait()
    wo = W[0].wait()
    for n in range(0, width, 256):
        after.ref[:, n : n + 256] = ar[:, n : n + 256] + dot(mr[...], wo[:, n : n + 256], 1, 0)
    after.start()
    norm_rows(after.ref, normed.ref, gb.wait(), 2, 1024)
    normed.start()
    wt = W[1].wait()
    I.later()
    nr = normed.ref[...]
    for n in range(0, hidden, 256):
        h = dot(nr, wt[n : n + 256, :], 1, 1)
        cdf = 0.5 + 0.5 * lax.erf(h * (0.5**0.5))
        active.ref[:, n : n + 256] = (h * cdf).astype(BF16)
        bell = jnp.exp(h * h * -0.5) * (0.5 / np.pi) ** 0.5
        slope.ref[:, n : n + 256] = (cdf + h * bell).astype(BF16)
        if (n + 256) % 768 == 0:
            active.start(n // 768)
    slope.start()


def weight_grad(dst, left, right, step=768):
    rows = dst.ref.shape[0]
    blocks = isinstance(dst, Blocks)
    for n in range(0, rows, step):
        dst.ref[n : n + step, :] = dot(left[:, n : n + step], right[...], 0, 0).astype(BF16)
        if blocks:
            dst.start(n + step)
    if not blocks:
        dst.start()


def ffn_out_grad(sm, I, W, O, G, X):
    (ints,) = sm
    active, cot = I
    (g3,) = O
    (wide,) = X
    put(wide, 0, 0, cot.wait()[...].astype(F32))
    n_seq, n_col = ints[0], ints[1]

    def take(t, rows):
        at = lax.broadcasted_iota(jnp.int32, (256, 1), 0) + t
        keep = ((at % 32 < n_seq) & (at // 32 < n_col)).astype(F32)
        g3.ref[t : t + 256, :] = (rows * keep).astype(BF16)

    to_columns(wide, take)
    g3.start()
    weight_grad(G[0], active.wait(), g3.ref)


def ffn_back(sm, I, W, O, G, X):
    g3, slope, normed = I
    (grad_hidden,) = O
    wf = W[0].wait()
    gr, sl = g3.wait(), slope.wait()
    I.later()
    gh = grad_hidden.ref
    hidden = gh.shape[1]
    gv = gr[...]
    for n in range(0, hidden, 256):
        d = dot(gv, wf[n : n + 256, :], 1, 1)
        gh[:, n : n + 256] = (d * sl[:, n : n + 256].astype(F32)).astype(BF16)
    grad_hidden.start()
    weight_grad(G[0], gh, normed.wait())


def ffn_result(sm, I, W, O, G, X):
    active, after = I
    layer_out = O[0]
    (res,) = X
    width = layer_out.ref.shape[1]
    wf = W[0].wait()
    ac, ar = active.wait(), after.wait()
    I.later()
    for n in range(0, width, 256):
        put(res, 0, n, ar[:, n : n + 256] + dot(ac[...], wf[:, n : n + 256], 1, 0))

    def take(t, rows):
        layer_out.ref[t : t + 256, :] = rows.astype(BF16)

    to_columns(res, take)
    layer_out.start()
    stamp(O[1])


def column_back(sm, I, W, O, G, X):
    grad_hidden, after_col, g3, gb = I
    grad_after, branch, grad_mixed, sums = O
    (dn,) = X
    g2, gm = branch.ref, grad_mixed.ref
    width = g2.shape[1]
    gh = grad_hidden.wait()
    wf = W[0].wait()
    I.later()
    for n in range(0, width, 256):
        dn[:, n : n + 256] = dot(gh[...], wf[:, n : n + 256], 1, 0)
    ac, base, g = after_col.wait(), g3.wait(), gb.wait()

    def emit(t, rows):
        grad_after.ref[t : t + 256, :] = rows
        g2[t : t + 256, :] = rows.astype(BF16)

    norm_back(dn, ac, base, g, 2, 1024, emit, sums.ref)
    grad_after.start()
    sums.start()
    wo = W[1].wait()
    for n in range(0, width, 256):
        gm[:, n : n + 256] = dot(g2[...], wo[n : n + 256, :], 1, 1).astype(BF16)
    grad_mixed.start()


def column_attend_back(sm, I, W, O, G, X):
    (ints,) = sm
    packed, grad_mixed = I
    gq = O[0]
    sc, dsc = X
    pr, gm = packed.wait(), grad_mixed.wait()
    I.later()
    width = gm.shape[1]
    halves = head_masks(128)
    out = gq.ref

    def scores(b, carry):
        rows = pl.ds(pl.multiple_of(b * 128, 128), 128)
        at = pl.ds(pl.multiple_of(b * 32, 32), 32)
        for lo in range(0, width, 128):
            qs = stacked(pr[rows, lo : lo + 128] * 0.125, halves)
            k = pr[rows, width + lo : width + lo + 128]
            v = pr[rows, 2 * width + lo : 2 * width + lo + 128]
            des = stacked(gm[rows, lo : lo + 128], halves)
            sc[at, 2 * lo : 2 * lo + 256] = pick_four(dot(k, qs, 1, 1))
            dsc[at, 2 * lo : 2 * lo + 256] = pick_four(dot(v, des, 1, 1))
        return carry

    lax.fori_loop(0, 8, scores, 0)
    column_softmax(sc, ints[0])

    def pull(b, carry):
        at = pl.ds(pl.multiple_of(b * 32, 32), 32)
        p, dp = sc[at, :], dsc[at, :]
        dsc[at, :] = p * (dp - jnp.sum(p * dp, 0, keepdims=True))
        return carry

    lax.fori_loop(0, 8, pull, 0)

    def spreads(b, carry):
        rows = pl.ds(pl.multiple_of(b * 128, 128), 128)
        at = pl.ds(pl.multiple_of(b * 32, 32), 32)
        for lo in range(0, width, 128):
            qs = stacked(pr[rows, lo : lo + 128] * 0.125, halves)
            k = pr[rows, width + lo : width + lo + 128]
            des = stacked(gm[rows, lo : lo + 128], halves)
            ds = spread_four(dsc[at, 2 * lo : 2 * lo + 256])
            dq = unstack(dot(ds, k, 0, 0)) * 0.125
            out[rows, lo : lo + 128] = dq.astype(BF16)
            out[rows, width + lo : width + lo + 128] = dot(ds, qs, 1, 0).astype(BF16)
            dv = dot(spread_four(sc[at, 2 * lo : 2 * lo + 256]), des, 1, 0)
            out[rows, 2 * width + lo : 2 * width + lo + 128] = dv.astype(BF16)
        return carry

    lax.fori_loop(0, 8, spreads, 0)
    gq.start()


def column_back_and_result(sm, I, W, O, G, X):
    attend, rest = Loads(), Loads()
    attend.extend(I[:2])
    rest.extend(I[2:])
    column_attend_back(sm, attend, W, O[:1], G, X[:2])
    ffn_result((), rest, W, O[1:], G, X[2:])


def product_grads(sm, I, W, O, G, X):
    I.later()
    for k, g in enumerate(G):
        weight_grad(g, I[2 * k].wait(), I[2 * k + 1].wait())


def row_back(sm, I, W, O, G, X):
    gq_col, after_row, grad_after, gb = I
    grad_row, branch, grad_mixed, sums = O
    dn, wide = X
    g1, gm = branch.ref, grad_mixed.ref
    width = g1.shape[1]
    wc = W[0].wait()
    gc = gq_col.wait()
    I.later()
    for n in range(0, width, 256):
        dn[:, n : n + 256] = dot(gc[...], wc[:, n : n + 256], 1, 0)
    ar, base, g = after_row.wait(), grad_after.wait(), gb.wait()

    def emit(t, rows):
        put(wide, t, 0, rows)

    norm_back(dn, ar, base, g, 1, 1024, emit, sums.ref)
    sums.start()

    def take(t, rows):
        grad_row.ref[t : t + 256, :] = rows
        g1[t : t + 256, :] = rows.astype(BF16)

    to_columns(wide, take)
    grad_row.start()
    wo = W[1].wait()
    for n in range(0, width, 256):
        gm[:, n : n + 256] = dot(g1[...], wo[n : n + 256, :], 1, 1).astype(BF16)
    grad_mixed.start()


def row_attend_back(sm, I, W, O, G, X):
    ints, flts = sm
    packed, grad_mixed, prob, logp, mixed, g1, normed, gb = I
    (gq,) = O
    (sc,) = X
    n_seq, n_col = ints[0], ints[1]
    pr, gm = packed.wait(), grad_mixed.wait()
    I.later()
    width = gm.shape[1]
    heads = width // HD
    halves = head_masks(512)
    for m in range(heads // 2):
        d, v = four(gm, m * 128), four(pr, 2 * width + m * 128)
        for e in range(2):
            h = 2 * m + e
            sc[h * 32 : (h + 1) * 32, :] = pick(dot(d * halves[e], v, 1, 1))
    p, lp = prob.wait()[...], logp.wait()[...]
    dp = sc[...]
    ent = jnp.sum(p * lp, -1, keepdims=True) * -0.25
    row = lax.broadcasted_iota(jnp.int32, ent.shape, 0) % 32
    w = jnp.where(row < n_col, penalty_weight / gb.wait()[6:7, 0:1], 0.0)
    ds = p * (dp - jnp.sum(p * dp, -1, keepdims=True) * 0.25) - w * p * (lp + ent)
    sc[...] = ds
    keep = (lax.broadcasted_iota(jnp.int32, (1024, 1), 0) // 32 < n_seq).astype(F32)
    scale = flts[0]
    out = gq.ref
    for m in range(heads // 2):
        lo = m * 128
        q, k, d = four(pr, lo), four(pr, width + lo), four(gm, lo)
        dq = dk = dv = 0.0
        for e in range(2):
            h = 2 * m + e
            pb = spread(prob.ref[h * 32 : (h + 1) * 32, :])
            sb = spread(sc[h * 32 : (h + 1) * 32, :])
            dq = dq + dot(sb, k * halves[e], 1, 0)
            dk = dk + dot(sb, q * halves[e], 0, 0)
            dv = dv + dot(pb, d * halves[e], 0, 0)
        for t in range(4):
            rows, lanes = slice(t * 256, (t + 1) * 256), slice(t * 128, (t + 1) * 128)
            out[rows, lo : lo + 128] = (
                dq[:, lanes] * (scale * keep[t * 256 : (t + 1) * 256])
            ).astype(BF16)
            out[rows, width + lo : width + lo + 128] = (dk[:, lanes] * scale).astype(BF16)
            out[rows, 2 * width + lo : 2 * width + lo + 128] = dv[:, lanes].astype(BF16)
    gq.start()
    weight_grad(G[0], mixed.wait(), g1.wait())
    weight_grad(G[1], out, normed.wait())


def input_back(sm, I, W, O, G, X):
    gq, x, grad_row, gb = I
    grad_in, sums = O
    (dn,) = X
    width = dn.shape[1]
    gr = gq.wait()
    wt = W[0].wait()
    I.later()
    for n in range(0, width, 256):
        dn[:, n : n + 256] = dot(gr[...], wt[:, n : n + 256], 1, 0)

    def emit(t, rows):
        grad_in.ref[t : t + 256, :] = rows

    norm_back(dn, x.wait(), grad_row.wait(), gb.wait(), 0, 1024, emit, sums.ref)
    grad_in.start()
    sums.start()


class Plan:
    def __init__(self, dp, fsdp, width):
        self.dp, self.fsdp, self.width = dp, fsdp, width
        self.fast = fsdp == 2 and dp == 16
        self.slots = dp * fsdp // 2
        if not self.fast:
            return
        place = [(z, x, c, y) for z in range(4) for x in range(2) for c in range(2) for y in range(2)]
        index = {p: n for n, p in enumerate(place)}

        def one(p):
            z, x, c, y = p
            return (z, 1 - x, c, y) if c == 0 else (z, x, c, 1 - y)

        def two(p):
            z, x, c, y = p
            return (z, 1 - x, c, y) if c == 1 else (z, x, c, 1 - y)

        def next_to(p):
            return (p[0] ^ 1, *p[1:])

        def across(p):
            return (p[0] ^ 2, *p[1:])

        def mate(p):
            return (p[0], p[1], 1 - p[2], p[3])

        def pairs(f):
            return [(n, index[f(p)]) for n, p in enumerate(place)]

        self.one, self.two, self.core = pairs(one), pairs(two), pairs(mate)
        self.next_to, self.across = pairs(next_to), pairs(across)
        gathered, owners = [], []
        for p in place:
            gathered.append([])
            for order in ((across, next_to, one, two), (one, across, next_to, two)):
                held = [p]
                for f in order:
                    held = held + [f(q) for q in held]
                gathered[-1].append([index[q] for q in held])
            owners.append([])
            for order in ((across, next_to, two, one), (two, across, next_to, one)):
                owned = [p]
                for f in order:
                    owned = owned + [f(q) for q in owned]
                owners[-1].append([index[q] for q in owned])
        mates = [index[mate(p)] for p in place]
        self.gather_tables = [
            np.array([gathered[n][k] + gathered[m][k] for n, m in enumerate(mates)], np.int32)
            for k in range(2)
        ]
        self.owner_tables = []
        for k in range(2):
            owned = np.array([owners[n][k] + owners[m][k] for n, m in enumerate(mates)], np.int32)
            self.owner_tables.append(np.argsort(owned, 1).astype(np.int32))

    def go(self, v, perm):
        return lax.ppermute(v, AXES, perm)

    def everywhere(self, v, beside):
        if not self.fast:
            return lax.psum(v, AXES)
        for perm in (self.core, self.one):
            v = v + lax.ppermute(v, AXES, perm)
        v = after(v, *beside.second_came)
        for perm in (self.two, self.next_to):
            v = v + lax.ppermute(v, AXES, perm)
        v = after(v, *beside.third_came)
        return v + lax.ppermute(v, AXES, self.across)


def after(v, *others):
    return lax.optimization_barrier((v, *others))[0]


class Gathering:
    def __init__(self, plan, shard):
        self.plan, self.have = plan, [shard[None]]

    def all(self, others):
        if others:
            self.have = list(lax.optimization_barrier((*self.have, *others)))[: len(self.have)]
        self.have = [jnp.concatenate(self.have, 0)] if len(self.have) > 1 else self.have
        return self.have[0]

    def step(self, perm, *others):
        self.came = self.plan.go(self.all(others), perm)
        self.have.append(self.came)
        return self.came

    def far(self, *others):
        self.mine = self.all(others)
        self.came = self.plan.go(self.mine, self.plan.two)
        return self.came

    def share(self, *others):
        mine = after(self.mine, *others) if others else self.mine
        self.mate = self.plan.go(mine, self.plan.core)
        return self.mate

    def last(self, *others):
        far = after(self.came, *others) if others else self.came
        self.end = self.plan.go(far, self.plan.core)
        return [self.mine, self.came, self.mate, self.end]


class Reduction:
    def __init__(self, plan, grads, names, shards):
        self.plan = plan
        self.names = [(n, shards[n].shape[0]) for n in names]
        if plan.fast:
            kept, self.sent = grads
            self.terms, self.size = [kept], kept.shape[0]
        else:
            self.whole = grads

    def go(self, v, perm):
        return lax.ppermute(v.astype(BF16), AXES, perm)

    def landed(self):
        return [self.came] if self.plan.fast else []

    def core(self, *others):
        if self.plan.fast:
            sent = after(self.sent, *others) if others else self.sent
            self.came = self.go(sent, self.plan.core)

    def total(self, start, stop):
        return sum(t[start:stop].astype(F32) for t in self.terms)

    def step(self, perm, *others):
        if self.plan.fast:
            came = after(self.came, *others) if others else self.came
            self.terms.append(came)
            self.size //= 2
            self.came = self.go(self.total(self.size, 2 * self.size), perm)

    def first(self, *others):
        self.step(self.plan.fast and self.plan.one, *others)

    def second(self, *others):
        self.step(self.plan.fast and self.plan.two, *others)

    def third(self, *others):
        self.second_came = self.landed()
        self.step(self.plan.fast and self.plan.next_to, *others)

    def fourth(self, *others):
        self.third_came = self.landed()
        self.step(self.plan.fast and self.plan.across, *others)

    def finish(self, *others):
        if self.plan.fast:
            self.terms.append(after(self.came, *others) if others else self.came)
            self.sum = self.total(0, 1)[0]

    def result(self):
        if self.plan.fast:
            cuts = np.cumsum([rows for _, rows in self.names])[:-1]
            return {n: v for (n, _), v in zip(self.names, jnp.split(self.sum, cuts, 0))}
        got = {}
        for (n, _), g in zip(self.names, self.whole):
            half = lax.psum_scatter(g, "dp", scatter_dimension=0, tiled=True)
            got[n] = lax.psum_scatter(half, "fsdp", scatter_dimension=1, tiled=True).astype(F32)
        return got


def local(
    plan,
    alignment_input,
    sequence_mask,
    column_length,
    output_cotangent,
    row_projection_weight,
    row_out_weight,
    column_projection_weight,
    column_out_weight,
    feedforward_in_weight,
    feedforward_out_weight,
    layer_norm_gain,
    layer_norm_bias,
):
    width = alignment_input.shape[3]
    tokens = alignment_input.shape[1] * alignment_input.shape[2]
    heads = width // HD
    hidden = feedforward_out_weight.shape[0] * plan.dp
    x = alignment_input.reshape(tokens, width)
    cot = output_cotangent.reshape(tokens, width)
    shards = dict(
        row_qkv=row_projection_weight.T,
        row_out=row_out_weight,
        col_qkv=column_projection_weight.T,
        col_out=column_out_weight,
        ffn_in=feedforward_in_weight.T,
        ffn_out=feedforward_out_weight,
    )
    whole_rows = {k: v.shape[0] * plan.dp for k, v in shards.items()}
    norms = jnp.concatenate([layer_norm_gain, layer_norm_bias], 0)
    share = norms.shape[1]
    devices = plan.dp * plan.fsdp
    me = lax.axis_index(AXES)
    n_seq = jnp.sum((sequence_mask > 0).astype(jnp.int32))
    n_col = column_length[0].astype(jnp.int32)
    ints = jnp.stack([n_seq, n_col])
    row_scale = 0.125 * lax.rsqrt(n_seq.astype(F32))

    w = {}
    if plan.fast:
        gather_row, early_row = (
            lax.dynamic_index_in_dim(jnp.asarray(t), me, 0, False) for t in plan.gather_tables
        )
        owner_row, first_row = (
            lax.dynamic_index_in_dim(jnp.asarray(t), me, 0, False) for t in plan.owner_tables
        )
        tables = [gather_row, owner_row, early_row]
        own_tables = dict(colg=[gather_row, first_row, early_row])
        extra = jnp.concatenate([norms.reshape(-1), n_col.astype(BF16)[None]])
        cols = shards["row_out"].shape[1]
        extra = jnp.pad(extra[None], ((0, 15), (0, cols - extra.shape[0])))
        groups = (("row_qkv",), ("row_out", "col_qkv"), ("col_out", "ffn_in"), ("ffn_out",))
        packs = []
        for gi, names in enumerate(groups):
            parts = [shards[n] for n in names] + ([extra] if gi == 0 else [])
            packs.append(jnp.concatenate(parts, 0) if len(parts) > 1 else parts[0])
        def ready(gi, bufs):
            row0 = 0
            for n in groups[gi]:
                rows = shards[n].shape[0]
                w[n] = Weights(bufs, row0, rows, whole_rows[n], width, True, 2 if gi == 3 else 0)
                row0 += rows
            return bufs

        late = []
        g1, g2, g3, g4 = (Gathering(plan, p) for p in packs)
        g1.step(plan.across)
        g4.step(plan.one)
        t = [g1.step(plan.next_to, g4.came, ints, *tables, first_row)]
        t = [g1.step(plan.one), g2.step(plan.across, *t)]
        t = [g1.far(*t), g2.step(plan.next_to, *t), g3.step(plan.across, *t)]
        g1.share(*t)
        bufs = ready(0, g1.last(*t))
        t = [g2.step(plan.one, *t), g3.step(plan.next_to, *t), g1.mate, g1.end]
        early = dict(rowf=t)
        slot = [g2.far(*t), g2.share(*t), g3.step(plan.one, *t), g4.step(plan.across, *t)]
        early["colf"] = slot

        def after_rowf(token):
            ready(1, g2.last(token, *slot))
            t = [token, *slot, g2.end]
            early["ffnf"] = [g3.far(*t), g3.share(*t), g4.step(plan.next_to, *t)]

        def after_colf(token):
            t = [token, *early["ffnf"]]
            ready(2, g3.last(*t))
            t = [token, g3.end]
            early["fout"] = [g4.far(*t), g4.share(*t)]

        hooks = dict(
            rowf=lambda outs: after_rowf(outs[5]),
            colf=lambda outs: after_colf(outs[1]),
            ffnf=lambda outs: late.append(ready(3, g4.last(outs[1], *early["fout"]))[3]),
        )
        rows = shards["row_qkv"].shape[0]
        w["norms"] = Weights(bufs, rows, 16, 16 * plan.dp, width, True)
        w["norms"].raw = True
    else:
        tables, own_tables = [jnp.zeros((1,), jnp.int32)] * 3, {}
        early, hooks, late = {}, {}, []
        for n, s in shards.items():
            half = lax.all_gather(s, "fsdp", axis=1, tiled=True)
            full = lax.all_gather(half, "dp", axis=0, tiled=True)
            w[n] = Weights([full], 0, s.shape[0], whole_rows[n], width, False)
        gb = lax.all_gather(norms, "fsdp", axis=1, tiled=True)
        gb = lax.all_gather(gb, "dp", axis=1, tiled=True).astype(F32)
        count = jnp.full((1, width), lax.psum(n_col.astype(F32), AXES))
        gb = jnp.concatenate([gb, count, jnp.zeros_like(count)], 0)
    flts = row_scale[None]

    micros = dict(
        rowf=9,
        colf=8,
        cola=4,
        ffnf=12,
        fout=7,
        ffnb=12,
        colb=10,
        colt=7,
        colg=7,
        rowb=10,
        rowt=13,
        inpb=9,
        lout=9,
    )

    def arr(n, dtype, rows=tokens, vmem=True, hbm=False):
        return Out((rows, n), dtype, vmem, hbm)

    resident = {}

    def run(name, body, smem, ins, weights, outs, grads=(), scratch=(), deps=(), fetch=()):
        ins = [a.bufs[0] if isinstance(a, Weights) else a for a in ins]
        weights = [w[n] if isinstance(n, str) else n for n in weights]
        fetch = [w[a] if isinstance(a, str) else Weights.of(a) for a in fetch]
        lists = own_tables.get(name, tables) + list(smem), ins, weights, outs, grads
        deps = list(deps) + early.get(name, [])
        got = fused(name, body, *lists, plan, resident, micros[name], scratch, deps, fetch)
        if name in hooks:
            hooks[name](got[0])
        return got

    wide = pltpu.VMEM((tokens, width), F32)
    turn = pltpu.VMEM((width // 128, 32 * PITCH + 8, 128), F32)
    score = pltpu.VMEM((heads * 32, 128), F32)
    flat = pltpu.VMEM((tokens // 4, 2 * width), F32)
    moment = arr(width, F32, 8, False, True)
    keep = dict(vmem=False, hbm=True)
    token = arr(128, F32, 8, **keep)

    (normed_row, packed_row, mixed_row, prob, logp, ent, gb), _ = run(
        "rowf",
        row_forward,
        [ints, flts],
        [x] if plan.fast else [x, gb],
        ["norms", "row_qkv"] if plan.fast else ["row_qkv"],
        [
            arr(width, BF16, **keep),
            arr(3 * width, BF16, **keep),
            arr(width, BF16, hbm=True),
            arr(128, F32, heads * 32, **keep),
            arr(128, F32, heads * 32, **keep),
            arr(width, F32, 8, **keep),
            arr(width, F32, 8, **keep),
        ],
        (),
        [score],
    )
    (after_row, normed_col, packed_col, mixed_col), _ = run(
        "colf",
        column_all,
        [ints],
        [x, mixed_row[0], gb],
        ["row_out", "col_qkv"],
        [
            arr(width, F32, hbm=True),
            arr(width, BF16, **keep),
            arr(3 * width, BF16, **keep),
            arr(width, BF16, hbm=True),
        ],
        (),
        [turn, flat],
    )
    (after_col, normed_ffn, active, slope, cot_here), _ = run(
        "ffnf",
        feed_forward,
        [],
        [after_row[0], mixed_col[0], gb],
        ["col_out", "ffn_in"],
        [
            arr(width, F32, **keep),
            arr(width, BF16, **keep),
            arr(hidden, BF16, hbm=True),
            arr(hidden, BF16),
        ],
        fetch=[cot],
    )
    (g3,), grads = run(
        "fout",
        ffn_out_grad,
        [ints],
        [active[0], cot_here],
        [],
        [arr(width, BF16)],
        [hidden],
        [turn],
    )
    r1 = Reduction(plan, grads, ["ffn_out"], shards)
    r1.core(*late)
    (grad_hidden, w_in, w_col_out, after_here), grads = run(
        "ffnb",
        ffn_back,
        [],
        [g3, slope, normed_ffn],
        ["ffn_out"],
        [arr(hidden, BF16)],
        [hidden],
        fetch=["ffn_in", "col_out", after_col],
    )
    r2 = Reduction(plan, grads, ["ffn_in"], shards)
    landed = r1.landed()
    r1.first(grads[0], *landed)
    r2.core(*landed)
    (grad_after, g2, gm_col, sums_two, packed_here, normed_here, mixed_here), _ = run(
        "colb",
        column_back,
        [],
        [grad_hidden, after_here, g3, gb],
        [w_in, w_col_out],
        [arr(width, F32, **keep), arr(width, BF16), arr(width, BF16), moment],
        (),
        [wide],
        landed,
        [packed_col, normed_col, mixed_col[1]],
    )
    landed = r1.landed() + r2.landed()
    r1.second(sums_two, *landed)
    r2.first(sums_two, *landed)
    (gq_col, layer_out, mark), _ = run(
        "colt",
        column_back_and_result,
        [ints],
        [packed_here, gm_col, active[1], after_col],
        ["ffn_out"],
        [arr(3 * width, BF16), arr(width, BF16, **keep), token],
        (),
        [flat, flat, turn],
        landed,
    )
    landed = r1.landed() + r2.landed()
    r1.third(mark, *landed)
    r2.second(mark, *landed)
    (w_col_qkv, w_row_out, after_row_here, grad_after_here), grads = run(
        "colg",
        product_grads,
        [],
        [gq_col, normed_here, mixed_here, g2],
        [],
        [],
        [3 * width, width],
        (),
        landed,
        ["col_qkv", "row_out", after_row[1], grad_after],
    )
    r3 = Reduction(plan, grads, ["col_qkv", "col_out"], shards)
    landed = r1.landed() + r2.landed()
    r1.fourth(grads[0], *landed)
    r2.third(grads[0], *landed)
    r3.core(*landed)
    (grad_row, g1, gm_row, sums_one, packed_here, normed_here, mixed_here), _ = run(
        "rowb",
        row_back,
        [],
        [gq_col, after_row_here, grad_after_here, gb],
        [w_col_qkv, w_row_out],
        [arr(width, F32, **keep), arr(width, BF16), arr(width, BF16), moment],
        (),
        [wide, turn],
        landed,
        [packed_row, normed_row, mixed_row[1]],
    )
    landed = r1.landed() + r2.landed() + r3.landed()
    r2.fourth(sums_one, *landed)
    r3.first(sums_one, *landed)
    (gq_row,), grads = run(
        "rowt",
        row_attend_back,
        [ints, flts],
        [packed_here, gm_row, prob, logp, mixed_here, g1, normed_here, gb],
        [],
        [arr(3 * width, BF16, **keep)],
        [width, 3 * width],
        [score],
        landed,
    )
    r4 = Reduction(plan, grads, ["row_out", "row_qkv"], shards)
    landed = r1.landed() + r2.landed() + r3.landed()
    r4.core(*landed)
    landed = landed + r4.landed()
    r1.finish()
    r2.finish()
    sums = [r.sum for r in (r1, r2)] if plan.fast else []
    r3.third(grads[0], *landed)
    r4.first(*landed, *sums)
    (grad_in, sums_zero), _ = run(
        "inpb",
        input_back,
        [],
        [gq_row, x, grad_row, gb],
        ["row_qkv"],
        [arr(width, F32, **keep), moment],
        (),
        [wide],
        [grads[0], *landed],
    )
    landed = r3.landed() + r4.landed()
    r4.second(sums_zero, *landed)
    r3.fourth(sums_zero, *landed)
    r4.third()
    landed = r4.landed()
    r3.second(*landed)
    r4.fourth()
    r3.finish()
    r4.finish(*([r3.sum] if plan.fast else []))
    got = {}
    for r in (r1, r2, r3, r4):
        got.update(r.result())
    sums_all = plan.everywhere(sums_zero + sums_one + sums_two + ent, r4)
    owned = lax.dynamic_slice_in_dim(sums_all[:6], me * share, share, 1)
    gains, biases = owned[0::2], owned[1::2]
    shape = alignment_input.shape
    return (
        layer_out.reshape(shape),
        grad_in.reshape(shape),
        got["row_qkv"].T,
        got["row_out"],
        got["col_qkv"].T,
        got["col_out"],
        got["ffn_in"].T,
        got["ffn_out"],
        gains,
        biases[:2],
        biases[2],
        sums_all[6, 0],
    )


def solution(mesh):
    def whole(*args):
        plan = Plan(mesh.shape["dp"], mesh.shape["fsdp"], args[0].shape[3])
        return jax.shard_map(
            lambda *blocks: local(plan, *blocks),
            mesh=mesh,
            in_specs=(
                P(AXES, None, None, None),
                P(AXES, None),
                P(AXES),
                P(AXES, None, None, None),
                P("fsdp", "dp"),
                P("dp", "fsdp"),
                P("fsdp", "dp"),
                P("dp", "fsdp"),
                P("fsdp", "dp"),
                P("dp", "fsdp"),
                P(None, AXES),
                P(None, AXES),
            ),
            out_specs=(
                P(AXES, None, None, None),
                P(AXES, None, None, None),
                P("fsdp", "dp"),
                P("dp", "fsdp"),
                P("fsdp", "dp"),
                P("dp", "fsdp"),
                P("fsdp", "dp"),
                P("dp", "fsdp"),
                P(None, AXES),
                P(None, AXES),
                P(AXES),
                P(),
            ),
            check_vma=False,
        )(*args)

    return whole
```

profile of v0, /device:TPU:0, one launch (start us, length us, event | category | flops | bytes accessed | tf_op | source)
XLA Modules:
  0.0 320.4 jit_solution(10597843608180260018)
XLA Ops:
  3.1 4.1 %collective-permute-start = (bf16[1,160,384]{2,1,0:T(8,128)(2,1)S(1)}, bf16[1,160,384]{2,1,0:T(8,128)(2,1)S(1)}, u32[]{:S(2)}, u32[]{:S(2)}) collective-permute-start(bf16[1,160,384]{2,1,0:T(8,128)(2,1)S(1)} %fusion.2), channel_id=1, source_target_pairs={{0,16},{1,17},{2,18},{3,19},{4,20},{5,21},{6,22},{7,23},{8,24},{9,... | collective-permute-start | bytes 368648 | tf_op jit(solution)/shard_map/ppermute | solution.py:897
  7.2 1.5 collective-permute-start.1
  8.7 1.3 fusion.7
  11.5 1.2 fusion.5
  15.0 6.0 %collective-permute-done.2 = bf16[2,160,384]{2,1,0:T(8,128)(2,1)S(1)} collective-permute-done((bf16[2,160,384]{2,1,0:T(8,128)(2,1)S(1)}, bf16[2,160,384]{2,1,0:T(8,128)(2,1)S(1)}, u32[]{:S(2)}, u32[]{:S(2)}) %collective-permute-start.2) | collective-permute-done | bytes 245792 | tf_op jit(solution)/shard_map/ppermute | solution.py:897
  21.1 1.3 collective-permute-start.3
  22.4 3.4 %collective-permute-start.4 = (bf16[1,192,384]{2,1,0:T(8,128)(2,1)S(1)}, bf16[1,192,384]{2,1,0:T(8,128)(2,1)S(1)}, u32[]{:S(2)}, u32[]{:S(2)}) collective-permute-start(bf16[1,192,384]{2,1,0:T(8,128)(2,1)S(1)} %maximum_bitcast_fusion.1), channel_id=1, source_target_pairs={{0,16},{1,17},{2,18},{3,19},{4,20},{5,21},{6,22},{7,23},{8,24},{9,... | collective-permute-start | bytes 442376 | tf_op jit(solution)/shard_map/ppermute | solution.py:897
  25.8 6.4 %collective-permute-done.4 = bf16[1,192,384]{2,1,0:T(8,128)(2,1)S(1)} collective-permute-done((bf16[1,192,384]{2,1,0:T(8,128)(2,1)S(1)}, bf16[1,192,384]{2,1,0:T(8,128)(2,1)S(1)}, u32[]{:S(2)}, u32[]{:S(2)}) %collective-permute-start.4) | collective-permute-done | bytes 147488 | tf_op jit(solution)/shard_map/ppermute | solution.py:897
  33.8 3.4 %collective-permute-start.7 = (bf16[1,240,384]{2,1,0:T(8,128)(2,1)S(1)}, bf16[1,240,384]{2,1,0:T(8,128)(2,1)S(1)}, u32[]{:S(2)}, u32[]{:S(2)}) collective-permute-start(bf16[1,240,384]{2,1,0:T(8,128)(2,1)S(1)} %maximum_bitcast_fusion), channel_id=1, source_target_pairs={{0,16},{1,17},{2,18},{3,19},{4,20},{5,21},{6,22},{7,23},{8,24},{9,... | collective-permute-start | bytes 552968 | tf_op jit(solution)/shard_map/ppermute | solution.py:897
  37.2 7.6 %collective-permute-done.7 = bf16[1,240,384]{2,1,0:T(8,128)(2,1)S(1)} collective-permute-done((bf16[1,240,384]{2,1,0:T(8,128)(2,1)S(1)}, bf16[1,240,384]{2,1,0:T(8,128)(2,1)S(1)}, u32[]{:S(2)}, u32[]{:S(2)}) %collective-permute-start.7) | collective-permute-done | bytes 184352 | tf_op jit(solution)/shard_map/ppermute | solution.py:897
  44.8 1.5 collective-permute-done.6
  47.1 1.6 collective-permute-start.10
  48.7 1.5 collective-permute-start.11
  50.3 8.5 %collective-permute-done.11.refs_11_ = bf16[2,240,384]{2,1,0:T(8,128)(2,1)S(1)} collective-permute-done((bf16[2,240,384]{2,1,0:T(8,128)(2,1)S(1)}, bf16[2,240,384]{2,1,0:T(8,128)(2,1)S(1)}, u32[]{:S(2)}, u32[]{:S(2)}) %collective-permute-start.11) | collective-permute-done | bytes 368672 | tf_op jit(solution)/shard_map/ppermute | solution.py:897
  60.8 1.7 collective-permute-start.12
  64.8 2.5 collective-permute-start.15
  67.9 11.9 %rowf.1 = (bf16[1024,768]{1,0:T(8,128)(2,1)}, bf16[1024,2304]{1,0:T(8,128)(2,1)}, bf16[1024,768]{1,0:T(8,128)(2,1)S(1)}, bf16[1024,768]{1,0:T(8,128)(2,1)}, f32[...) custom-call(s32[32]{0:T(128)S(1)} %get-tuple-element.230.refs_0_, ...), custom_call_target="tpu_custom_call" | custom-call | flops 9000000 | bytes 27000 | tf_op jit(solution)/shard_map/rowf/pallas_call | solution.py:218
  79.9 1.1 collective-permute-done.15.refs_14_
  80.9 2.8 collective-permute-done.14.refs_13_
  83.7 1.6 collective-permute-done.12.refs_8_.refs_11_
  85.3 3.1 collective-permute-done.16.refs_10_
  88.3 1.6 constant_dynamic-update-slice_fusion.18
  90.3 1.7 collective-permute-start.17
  92.1 1.5 collective-permute-start.19
  93.6 27.9 %colf.1 = (f32[1024,768]{1,0:T(8,128)S(1)}, f32[1024,768]{1,0:T(8,128)}, bf16[1024,768]{1,0:T(8,128)(2,1)}, bf16[1024,2304]{1,0:T(8,128)(2,1)}, bf16[1024,768]{1...) custom-call(s32[32]{0:T(128)S(1)} %get-tuple-element.230.refs_0_, s32[32]{0:T(128)S(1)} %get-tuple-element.231.refs_1_, ...), custom_call_target="tpu_custom_call" | custom-call | flops 8000000 | bytes 24000 | tf_op jit(solution)/shard_map/colf/pallas_call | solution.py:218
  121.7 3.3 %collective-permute-done.20.refs_9_.refs_13_ = bf16[8,240,384]{2,1,0:T(8,128)(2,1)S(1)} collective-permute-done((bf16[8,240,384]{2,1,0:T(8,128)(2,1)S(1)}, bf16[8,240,384]{2,1,0:T(8,128)(2,1)S(1)}, u32[]{:S(2)}, u32[]{:S(2)}) %collective-permute-start.20) | collective-permute-done | bytes 1474592 | tf_op jit(solution)/shard_map/ppermute | solution.py:897
  126.1 14.6 %ffnf.1 = (f32[1024,768]{1,0:T(8,128)}, bf16[1024,768]{1,0:T(8,128)(2,1)}, bf16[1024,3072]{1,0:T(8,128)(2,1)S(1)}, bf16[1024,3072]{1,0:T(8,128)(2,1)}, bf16[1024...) custom-call(s32[32]{0:T(128)S(1)} %get-tuple-element.230.refs_0_, s32[32]{0:T(128)S(1)} %get-tuple-element.231.refs_1_, ...), custom_call_target="tpu_custom_call" | custom-call | flops 12000000 | bytes 36000 | tf_op jit(solution)/shard_map/ffnf/pallas_call | solution.py:218
  141.6 7.7 %fout.1 = (bf16[1024,768]{1,0:T(8,128)(2,1)S(1)}, bf16[16,192,384]{2,1,0:T(8,128)(2,1)}, bf16[16,192,384]{2,1,0:T(8,128)(2,1)}) custom-call(s32[32]{0:T(128)S(1)} %get-tuple-element.230.refs_0_, s32[32]{0:T(128)S(1)} %get-tuple-element.231.refs_1_, s32[32]{0:T(128)S(1)} %get-tuple-element.232.refs_2_, s32[2]{0:T(128)S(1)} %pad_add_fusion.refs_3_, ...), custom_call_target="tpu_custom_call" | custom-call | flops 7000000 | bytes 21000 | tf_op jit(solution)/shard_map/fout/pallas_call | solution.py:218
  150.3 15.9 %ffnb.1 = (bf16[1024,3072]{1,0:T(8,128)(2,1)S(1)}, bf16[3072,768]{1,0:T(8,128)(2,1)S(1)}, bf16[768,768]{1,0:T(8,128)(2,1)S(1)}, f32[1024,768]{1,0:T(8,128)S(1)},...) custom-call(s32[32]{0:T(128)S(1)} %get-tuple-element.230.refs_0_, s32[32]{0:T(128)S(1)} %get-tuple-element.231.refs_1_, ...), custom_call_target="tpu_custom_call" | custom-call | flops 12000000 | bytes 36000 | tf_op jit(solution)/shard_map/ffnb/pallas_call | solution.py:218
  168.0 12.1 %colb.1 = (f32[1024,768]{1,0:T(8,128)}, bf16[1024,768]{1,0:T(8,128)(2,1)S(1)}, bf16[1024,768]{1,0:T(8,128)(2,1)S(1)}, f32[8,768]{1,0:T(8,128)}, bf16[1024,2304]{...) custom-call(s32[32]{0:T(128)S(1)} %get-tuple-element.230.refs_0_, ...), custom_call_target="tpu_custom_call" | custom-call | flops 10000000 | bytes 30000 | tf_op jit(solution)/shard_map/colb/pallas_call | solution.py:218
  180.1 3.3 %collective-permute-done.25.refs_12_ = bf16[8,192,384]{2,1,0:T(8,128)(2,1)S(1)} collective-permute-done((bf16[8,192,384]{2,1,0:T(8,128)(2,1)S(1)}, bf16[8,192,384]{2,1,0:T(8,128)(2,1)S(1)}, u32[]{:S(2)}, u32[]{:S(2)}) %collective-permute-start.25) | collective-permute-done | bytes 1179680 | tf_op jit(solution)/shard_map/ppermute | solution.py:957
  185.9 15.6 %colt.1 = (bf16[1024,2304]{1,0:T(8,128)(2,1)S(1)}, bf16[1024,768]{1,0:T(8,128)(2,1)}, f32[8,128]{1,0:T(8,128)}) custom-call(s32[32]{0:T(128)S(1)} %get-tuple-element.230.refs_0_, s32[32]{0:T(128)S(1)} %get-tuple-element.231.refs_1_, s32[32]{0:T(128)S(1)} %get-tuple-element.232.refs_2_, s32[2]{0:T(128)S(1)} %pad_add_fusion.refs_3_, ...), custom_call_target="tpu_custom_call" | custom-call | flops 7000000 | bytes 21000 | tf_op jit(solution)/shard_map/colt/pallas_call | solution.py:218
  201.5 3.7 %collective-permute-done.28.refs_14_ = bf16[8,192,384]{2,1,0:T(8,128)(2,1)S(1)} collective-permute-done((bf16[8,192,384]{2,1,0:T(8,128)(2,1)S(1)}, bf16[8,192,384]{2,1,0:T(8,128)(2,1)S(1)}, u32[]{:S(2)}, u32[]{:S(2)}) %collective-permute-start.28) | collective-permute-done | bytes 1179680 | tf_op jit(solution)/shard_map/ppermute | solution.py:957
  205.5 1.5 collective-permute-start.30
  206.9 1.1 add_convert_fusion.11
  208.6 9.4 %colg.1 = (bf16[2304,768]{1,0:T(8,128)(2,1)S(1)}, bf16[768,768]{1,0:T(8,128)(2,1)S(1)}, f32[1024,768]{1,0:T(8,128)S(1)}, f32[1024,768]{1,0:T(8,128)S(1)}, bf16[1...) custom-call(s32[32]{0:T(128)S(1)} %get-tuple-element.230.refs_0_, s32[32]{0:T(128)S(1)} %copy-done.13, ...), custom_call_target="tpu_custom_call" | custom-call | flops 7000000 | bytes 21000 | tf_op jit(solution)/shard_map/colg/pallas_call | solution.py:218
  218.4 1.6 collective-permute-start.32
  221.0 2.0 collective-permute-start.31
  222.9 11.5 %rowb.1 = (f32[1024,768]{1,0:T(8,128)}, bf16[1024,768]{1,0:T(8,128)(2,1)S(1)}, bf16[1024,768]{1,0:T(8,128)(2,1)S(1)}, f32[8,768]{1,0:T(8,128)}, bf16[1024,2304]{...) custom-call(s32[32]{0:T(128)S(1)} %get-tuple-element.230.refs_0_, ...), custom_call_target="tpu_custom_call" | custom-call | flops 10000000 | bytes 30000 | tf_op jit(solution)/shard_map/rowb/pallas_call | solution.py:218
  234.8 1.5 collective-permute-start.35
  237.7 12.5 %rowt.1 = (bf16[1024,2304]{1,0:T(8,128)(2,1)}, bf16[16,192,384]{2,1,0:T(8,128)(2,1)}, bf16[16,192,384]{2,1,0:T(8,128)(2,1)}) custom-call(s32[32]{0:T(128)S(1)} %get-tuple-element.230.refs_0_, s32[32]{0:T(128)S(1)} %get-tuple-element.231.refs_1_, s32[32]{0:T(128)S(1)} %get-tuple-element.232.refs_2_, s32[2]{0:T(128)S(1)} %pad_add_fusion.refs_3_, ...), custom_call_target="tpu_custom_call" | custom-call | flops 13000000 | bytes 39000 | tf_op jit(solution)/shard_map/rowt/pallas_call | solution.py:218
  251.1 1.9 add_bitcast_fusion.1
  253.0 2.9 collective-permute-done.36.refs_15_
  255.9 2.4 add_convert_fusion
  258.3 1.5 collective-permute-start.37
  260.4 11.8 %inpb.1 = (f32[1024,768]{1,0:T(8,128)}, f32[8,768]{1,0:T(8,128)}) custom-call(s32[32]{0:T(128)S(1)} %get-tuple-element.230.refs_0_, s32[32]{0:T(128)S(1)} %get-tuple-element.231.refs_1_, s32[32]{0:T(128)S(1)} %get-tuple-element.232.refs_2_, bf16[1024,2304]{1,0:T(8,128)(2,1)} %get-tuple-element.213.refs_3_, bf16[1024,768]{1,0:T(8,128)(2,1)} %bitcast.48, ...), custom_call_target="tpu_custom_call" | custom-call | flops 9000000 | bytes 27000 | tf_op jit(solution)/shard_map/inpb/pallas_call | solution.py:218
  272.3 2.5 collective-permute-done.38
  276.2 1.2 collective-permute-done.44
  277.4 1.4 collective-permute-start.45
  278.8 6.4 %collective-permute-done.39 = bf16[4,192,384]{2,1,0:T(8,128)(2,1)S(1)} collective-permute-done((bf16[4,192,384]{2,1,0:T(8,128)(2,1)S(1)}, bf16[4,192,384]{2,1,0:T(8,128)(2,1)S(1)}, u32[]{:S(2)}, u32[]{:S(2)}) %collective-permute-start.39) | collective-permute-done | bytes 589856 | tf_op jit(solution)/shard_map/ppermute | solution.py:957
  286.6 1.9 add_convert_fusion.8
  288.4 1.6 collective-permute-start.42
  290.6 1.2 collective-permute-start.46
  291.8 2.9 collective-permute-done.46
  295.5 1.7 collective-permute-start.47
  297.2 1.9 add_bitcast_fusion
  299.4 3.7 %collective-permute-done.42 = bf16[2,192,384]{2,1,0:T(8,128)(2,1)} collective-permute-done((bf16[2,192,384]{2,1,0:T(8,128)(2,1)}, bf16[2,192,384]{2,1,0:T(8,128)(2,1)}, u32[]{:S(2)}, u32[]{:S(2)}) %collective-permute-start.42) | collective-permute-done | bytes 294944 | tf_op jit(solution)/shard_map/ppermute | solution.py:957
  303.0 1.3 add_convert_fusion.12
  304.3 1.3 add_convert_fusion.13
  305.6 3.0 collective-permute-start.41
  308.6 1.1 collective-permute-start.43
  312.0 2.9 collective-permute-done.41
  314.9 1.3 convert_add_fusion.1
  317.5 1.3 convert_add_fusion
  (204 shorter events, 34.5 us)
Async XLA Ops:
  0.6 21.7 %copy-start.37 = (bf16[384,144]{0,1:T(8,128)(2,1)S(1)}, bf16[384,144]{0,1:T(8,128)(2,1)}, u32[]{:S(2)}) copy-start(bf16[384,144]{0,1:T(8,128)(2,1)} %param.22) | copy-start | bytes 331780
  0.7 21.7 %copy-start.38 = (bf16[48,384]{1,0:T(8,128)(2,1)S(1)}, bf16[48,384]{1,0:T(8,128)(2,1)}, u32[]{:S(2)}) copy-start(bf16[48,384]{1,0:T(8,128)(2,1)} %param.21) | copy-start | bytes 110596
  3.1 10.1 %collective-permute-start = (bf16[1,160,384]{2,1,0:T(8,128)(2,1)S(1)}, bf16[1,160,384]{2,1,0:T(8,128)(2,1)S(1)}, u32[]{:S(2)}, u32[]{:S(2)}) collective-permute-start(bf16[1,160,384]{2,1,0:T(8,128)(2,1)S(1)} %fusion.2), channel_id=1, source_target_pairs={{0,16},{1,17},{2,18},{3,19},{4,20},{5,21},{6,22},{7,23},{8,24},{9,... | collective-permute-start | bytes 368648 | tf_op jit(solution)/shard_map/ppermute | solution.py:897
  7.2 6.0 %collective-permute-start.1 = (bf16[1,192,384]{2,1,0:T(8,128)(2,1)}, bf16[1,192,384]{2,1,0:T(8,128)(2,1)S(1)}, u32[]{:S(2)}, u32[]{:S(2)}) collective-permute-start(bf16[1,192,384]{2,1,0:T(8,128)(2,1)} %bitcast.50), channel_id=1, source_target_pairs={{0,4},{1,5},{2,3},{3,2},{4,0},{5,1},{6,7},{7,6},{8,12},{9,13},{10,... | collective-permute-start | bytes 442376 | tf_op jit(solution)/shard_map/ppermute | solution.py:897
  13.9 7.1 %collective-permute-start.2 = (bf16[2,160,384]{2,1,0:T(8,128)(2,1)S(1)}, bf16[2,160,384]{2,1,0:T(8,128)(2,1)S(1)}, u32[]{:S(2)}, u32[]{:S(2)}) collective-permute-start(bf16[2,160,384]{2,1,0:T(8,128)(2,1)S(1)} %pad_maximum_fusion), channel_id=1, source_target_pairs={{0,8},{1,9},{2,10},{3,11},{4,12},{5,13},{6,14},{7,15},{8,0},{9,1},... | collective-permute-start | bytes 737288 | tf_op jit(solution)/shard_map/ppermute | solution.py:897
  15.0 18.8 %copy-start.36 = (bf16[384,192]{0,1:T(8,128)(2,1)S(1)}, bf16[384,192]{0,1:T(8,128)(2,1)}, u32[]{:S(2)}) copy-start(bf16[384,192]{0,1:T(8,128)(2,1)} %param.24) | copy-start | bytes 442372
  15.0 18.8 %copy-start.39 = (bf16[48,384]{1,0:T(8,128)(2,1)S(1)}, bf16[48,384]{1,0:T(8,128)(2,1)}, u32[]{:S(2)}) copy-start(bf16[48,384]{1,0:T(8,128)(2,1)} %param.23) | copy-start | bytes 110596
  21.1 11.2 %collective-permute-start.3 = (bf16[4,160,384]{2,1,0:T(8,128)(2,1)S(1)}, bf16[4,160,384]{2,1,0:T(8,128)(2,1)S(1)}, u32[]{:S(2)}, u32[]{:S(2)}) collective-permute-start(bf16[4,160,384]{2,1,0:T(8,128)(2,1)S(1)} %constant_dynamic-update-slice_fusion), channel_id=1, source_target_pairs={{0,4},{1,5},{2,3},{3,2},{4,0},{5,1},{6,7},{7,6},{8,12},{9,13},{10,... | collective-permute-start | bytes 1474568 | tf_op jit(solution)/shard_map/ppermute | solution.py:897
  22.4 9.8 %collective-permute-start.4 = (bf16[1,192,384]{2,1,0:T(8,128)(2,1)S(1)}, bf16[1,192,384]{2,1,0:T(8,128)(2,1)S(1)}, u32[]{:S(2)}, u32[]{:S(2)}) collective-permute-start(bf16[1,192,384]{2,1,0:T(8,128)(2,1)S(1)} %maximum_bitcast_fusion.1), channel_id=1, source_target_pairs={{0,16},{1,17},{2,18},{3,19},{4,20},{5,21},{6,22},{7,23},{8,24},{9,... | collective-permute-start | bytes 442376 | tf_op jit(solution)/shard_map/ppermute | solution.py:897
  32.4 26.4 %copy-start.20 = (bf16[8,160,384]{2,1,0:T(8,128)(2,1)}, bf16[8,160,384]{2,1,0:T(8,128)(2,1)S(1)}, u32[]{:S(2)}) copy-start(bf16[8,160,384]{2,1,0:T(8,128)(2,1)S(1)} %constant_dynamic-update-slice_fusion.3.refs_6_.refs_7_) | copy-start | bytes 2949124
  32.4 14.2 %collective-permute-start.5 = (bf16[8,160,384]{2,1,0:T(8,128)(2,1)S(1)}, bf16[8,160,384]{2,1,0:T(8,128)(2,1)S(1)}, u32[]{:S(2)}, u32[]{:S(2)}) collective-permute-start(bf16[8,160,384]{2,1,0:T(8,128)(2,1)S(1)} %constant_dynamic-update-slice_fusion.3.refs_6_.refs_7_), channel_id=1, source_target_pairs={{0,1},{1,0},{2,6},{3,7},{4,5},{5,4},{6,2},{7,3},{8,9},{9,8},{10,14... | collective-permute-start | bytes 2949128 | tf_op jit(solution)/shard_map/ppermute | solution.py:897
  33.0 13.3 %collective-permute-start.6 = (bf16[2,192,384]{2,1,0:T(8,128)(2,1)S(1)}, bf16[2,192,384]{2,1,0:T(8,128)(2,1)S(1)}, u32[]{:S(2)}, u32[]{:S(2)}) collective-permute-start(bf16[2,192,384]{2,1,0:T(8,128)(2,1)S(1)} %constant_dynamic-update-slice_fusion.5), channel_id=1, source_target_pairs={{0,8},{1,9},{2,10},{3,11},{4,12},{5,13},{6,14},{7,15},{8,0},{9,1},... | collective-permute-start | bytes 884744 | tf_op jit(solution)/shard_map/ppermute | solution.py:897
  33.8 11.0 %collective-permute-start.7 = (bf16[1,240,384]{2,1,0:T(8,128)(2,1)S(1)}, bf16[1,240,384]{2,1,0:T(8,128)(2,1)S(1)}, u32[]{:S(2)}, u32[]{:S(2)}) collective-permute-start(bf16[1,240,384]{2,1,0:T(8,128)(2,1)S(1)} %maximum_bitcast_fusion), channel_id=1, source_target_pairs={{0,16},{1,17},{2,18},{3,19},{4,20},{5,21},{6,22},{7,23},{8,24},{9,... | collective-permute-start | bytes 552968 | tf_op jit(solution)/shard_map/ppermute | solution.py:897
  46.5 12.2 %copy-start.24 = (bf16[8,160,384]{2,1,0:T(8,128)(2,1)}, bf16[8,160,384]{2,1,0:T(8,128)(2,1)S(1)}, u32[]{:S(2)}) copy-start(bf16[8,160,384]{2,1,0:T(8,128)(2,1)S(1)} %collective-permute-done.5.refs_7_.refs_8_) | copy-start | bytes 2949124
  46.5 12.2 %collective-permute-start.8 = (bf16[8,160,384]{2,1,0:T(8,128)(2,1)S(1)}, bf16[8,160,384]{2,1,0:T(8,128)(2,1)S(1)}, u32[]{:S(2)}, u32[]{:S(2)}) collective-permute-start(bf16[8,160,384]{2,1,0:T(8,128)(2,1)S(1)} %constant_dynamic-update-slice_fusion.3.refs_6_.refs_7_), channel_id=1, source_target_pairs={{0,2},{1,3},{2,0},{3,1},{4,6},{5,7},{6,4},{7,5},{8,10},{9,11},{10,... | collective-permute-start | bytes 2949128 | tf_op jit(solution)/shard_map/ppermute | solution.py:897
  46.5 12.2 %collective-permute-start.9 = (bf16[8,160,384]{2,1,0:T(8,128)(2,1)S(1)}, bf16[8,160,384]{2,1,0:T(8,128)(2,1)}, u32[]{:S(2)}, u32[]{:S(2)}) collective-permute-start(bf16[8,160,384]{2,1,0:T(8,128)(2,1)S(1)} %collective-permute-done.5.refs_7_.refs_8_), channel_id=1, source_target_pairs={{0,2},{1,3},{2,0},{3,1},{4,6},{5,7},{6,4},{7,5},{8,10},{9,11},{10,... | collective-permute-start | bytes 2949128 | tf_op jit(solution)/shard_map/ppermute | solution.py:897
  47.1 11.6 %collective-permute-start.10 = (bf16[4,192,384]{2,1,0:T(8,128)(2,1)S(1)}, bf16[4,192,384]{2,1,0:T(8,128)(2,1)S(1)}, u32[]{:S(2)}, u32[]{:S(2)}) collective-permute-start(bf16[4,192,384]{2,1,0:T(8,128)(2,1)S(1)} %constant_dynamic-update-slice_fusion.7), channel_id=1, source_target_pairs={{0,4},{1,5},{2,3},{3,2},{4,0},{5,1},{6,7},{7,6},{8,12},{9,13},{10,... | collective-permute-start | bytes 1769480 | tf_op jit(solution)/shard_map/ppermute | solution.py:897
  48.7 10.0 %collective-permute-start.11 = (bf16[2,240,384]{2,1,0:T(8,128)(2,1)S(1)}, bf16[2,240,384]{2,1,0:T(8,128)(2,1)S(1)}, u32[]{:S(2)}, u32[]{:S(2)}) collective-permute-start(bf16[2,240,384]{2,1,0:T(8,128)(2,1)S(1)} %constant_dynamic-update-slice_fusion.9), channel_id=1, source_target_pairs={{0,8},{1,9},{2,10},{3,11},{4,12},{5,13},{6,14},{7,15},{8,0},{9,1},... | collective-permute-start | bytes 1105928 | tf_op jit(solution)/shard_map/ppermute | solution.py:897
  60.8 22.8 %collective-permute-start.13 = (bf16[8,192,384]{2,1,0:T(8,128)(2,1)}, bf16[8,192,384]{2,1,0:T(8,128)(2,1)S(1)}, u32[]{:S(2)}, u32[]{:S(2)}) collective-permute-start(bf16[8,192,384]{2,1,0:T(8,128)(2,1)} %constant_dynamic-update-slice_fusion.11.refs_7_), channel_id=1, source_target_pairs={{0,2},{1,3},{2,0},{3,1},{4,6},{5,7},{6,4},{7,5},{8,10},{9,11},{10,... | collective-permute-start | bytes 3538952 | tf_op jit(solution)/shard_map/ppermute | solution.py:897
  60.8 24.4 %collective-permute-start.12 = (bf16[8,192,384]{2,1,0:T(8,128)(2,1)}, bf16[8,192,384]{2,1,0:T(8,128)(2,1)}, u32[]{:S(2)}, u32[]{:S(2)}) collective-permute-start(bf16[8,192,384]{2,1,0:T(8,128)(2,1)} %constant_dynamic-update-slice_fusion.11.refs_7_), channel_id=1, source_target_pairs={{0,1},{1,0},{2,6},{3,7},{4,5},{5,4},{6,2},{7,3},{8,9},{9,8},{10,14... | collective-permute-start | bytes 3538952 | tf_op jit(solution)/shard_map/ppermute | solution.py:897
  64.1 19.6 %collective-permute-start.14 = (bf16[4,240,384]{2,1,0:T(8,128)(2,1)}, bf16[4,240,384]{2,1,0:T(8,128)(2,1)S(1)}, u32[]{:S(2)}, u32[]{:S(2)}) collective-permute-start(bf16[4,240,384]{2,1,0:T(8,128)(2,1)} %constant_dynamic-update-slice_fusion.13), channel_id=1, source_target_pairs={{0,4},{1,5},{2,3},{3,2},{4,0},{5,1},{6,7},{7,6},{8,12},{9,13},{10,... | collective-permute-start | bytes 2211848 | tf_op jit(solution)/shard_map/ppermute | solution.py:897
  64.8 15.1 %copy-start.29 = (bf16[2,192,384]{2,1,0:T(8,128)(2,1)}, bf16[2,192,384]{2,1,0:T(8,128)(2,1)S(1)}, u32[]{:S(2)}) copy-start(bf16[2,192,384]{2,1,0:T(8,128)(2,1)S(1)} %constant_dynamic-update-slice_fusion.15) | copy-start | bytes 884740
  64.8 16.1 %collective-permute-start.15 = (bf16[2,192,384]{2,1,0:T(8,128)(2,1)S(1)}, bf16[2,192,384]{2,1,0:T(8,128)(2,1)S(1)}, u32[]{:S(2)}, u32[]{:S(2)}) collective-permute-start(bf16[2,192,384]{2,1,0:T(8,128)(2,1)S(1)} %constant_dynamic-update-slice_fusion.15), channel_id=1, source_target_pairs={{0,16},{1,17},{2,18},{3,19},{4,20},{5,21},{6,22},{7,23},{8,24},{9,... | collective-permute-start | bytes 884744 | tf_op jit(solution)/shard_map/ppermute | solution.py:897
  85.3 3.1 collective-permute-start.16
  90.1 31.5 %copy-start.17 = (bf16[8,240,384]{2,1,0:T(8,128)(2,1)}, bf16[8,240,384]{2,1,0:T(8,128)(2,1)S(1)}, u32[]{:S(2)}) copy-start(bf16[8,240,384]{2,1,0:T(8,128)(2,1)S(1)} %constant_dynamic-update-slice_fusion.17.refs_6_.refs_10_) | copy-start | bytes 4423684
  90.1 31.5 %collective-permute-start.18 = (bf16[8,240,384]{2,1,0:T(8,128)(2,1)S(1)}, bf16[8,240,384]{2,1,0:T(8,128)(2,1)S(1)}, u32[]{:S(2)}, u32[]{:S(2)}) collective-permute-start(bf16[8,240,384]{2,1,0:T(8,128)(2,1)S(1)} %constant_dynamic-update-slice_fusion.17.refs_6_.refs_10_), channel_id=1, source_target_pairs={{0,2},{1,3},{2,0},{3,1},{4,6},{5,7},{6,4},{7,5},{8,10},{9,11},{10,... | collective-permute-start | bytes 4423688 | tf_op jit(solution)/shard_map/ppermute | solution.py:897
  90.3 31.3 %collective-permute-start.17 = (bf16[8,240,384]{2,1,0:T(8,128)(2,1)S(1)}, bf16[8,240,384]{2,1,0:T(8,128)(2,1)S(1)}, u32[]{:S(2)}, u32[]{:S(2)}) collective-permute-start(bf16[8,240,384]{2,1,0:T(8,128)(2,1)S(1)} %constant_dynamic-update-slice_fusion.17.refs_6_.refs_10_), channel_id=1, source_target_pairs={{0,1},{1,0},{2,6},{3,7},{4,5},{5,4},{6,2},{7,3},{8,9},{9,8},{10,14... | collective-permute-start | bytes 4423688 | tf_op jit(solution)/shard_map/ppermute | solution.py:897
  92.1 29.5 %collective-permute-start.19 = (bf16[4,192,384]{2,1,0:T(8,128)(2,1)S(1)}, bf16[4,192,384]{2,1,0:T(8,128)(2,1)S(1)}, u32[]{:S(2)}, u32[]{:S(2)}) collective-permute-start(bf16[4,192,384]{2,1,0:T(8,128)(2,1)S(1)} %constant_dynamic-update-slice_fusion.19), channel_id=1, source_target_pairs={{0,8},{1,9},{2,10},{3,11},{4,12},{5,13},{6,14},{7,15},{8,0},{9,1},... | collective-permute-start | bytes 1769480 | tf_op jit(solution)/shard_map/ppermute | solution.py:897
  121.6 3.3 %collective-permute-start.20 = (bf16[8,240,384]{2,1,0:T(8,128)(2,1)S(1)}, bf16[8,240,384]{2,1,0:T(8,128)(2,1)S(1)}, u32[]{:S(2)}, u32[]{:S(2)}) collective-permute-start(bf16[8,240,384]{2,1,0:T(8,128)(2,1)S(1)} %collective-permute-done.17.refs_7_.refs_11_), channel_id=1, source_target_pairs={{0,2},{1,3},{2,0},{3,1},{4,6},{5,7},{6,4},{7,5},{8,10},{9,11},{10,... | collective-permute-start | bytes 4423688 | tf_op jit(solution)/shard_map/ppermute | solution.py:897
  125.1 15.5 %copy-start.19 = (bf16[8,192,384]{2,1,0:T(8,128)(2,1)}, bf16[8,192,384]{2,1,0:T(8,128)(2,1)S(1)}, u32[]{:S(2)}) copy-start(bf16[8,192,384]{2,1,0:T(8,128)(2,1)S(1)} %constant_dynamic-update-slice_fusion.21.refs_6_.refs_8_) | copy-start | bytes 3538948
  125.1 15.5 %collective-permute-start.22 = (bf16[8,192,384]{2,1,0:T(8,128)(2,1)S(1)}, bf16[8,192,384]{2,1,0:T(8,128)(2,1)S(1)}, u32[]{:S(2)}, u32[]{:S(2)}) collective-permute-start(bf16[8,192,384]{2,1,0:T(8,128)(2,1)S(1)} %constant_dynamic-update-slice_fusion.21.refs_6_.refs_8_), channel_id=1, source_target_pairs={{0,2},{1,3},{2,0},{3,1},{4,6},{5,7},{6,4},{7,5},{8,10},{9,11},{10,... | collective-permute-start | bytes 3538952 | tf_op jit(solution)/shard_map/ppermute | solution.py:897
  125.3 16.2 %collective-permute-start.21 = (bf16[8,192,384]{2,1,0:T(8,128)(2,1)S(1)}, bf16[8,192,384]{2,1,0:T(8,128)(2,1)S(1)}, u32[]{:S(2)}, u32[]{:S(2)}) collective-permute-start(bf16[8,192,384]{2,1,0:T(8,128)(2,1)S(1)} %constant_dynamic-update-slice_fusion.21.refs_6_.refs_8_), channel_id=1, source_target_pairs={{0,1},{1,0},{2,6},{3,7},{4,5},{5,4},{6,2},{7,3},{8,9},{9,8},{10,14... | collective-permute-start | bytes 3538952 | tf_op jit(solution)/shard_map/ppermute | solution.py:897
  141.6 7.7 %collective-permute-start.23 = (bf16[8,192,384]{2,1,0:T(8,128)(2,1)S(1)}, bf16[8,192,384]{2,1,0:T(8,128)(2,1)S(1)}, u32[]{:S(2)}, u32[]{:S(2)}) collective-permute-start(bf16[8,192,384]{2,1,0:T(8,128)(2,1)S(1)} %collective-permute-done.21.refs_6_.refs_7_.refs_9_), channel_id=1, source_target_pairs={{0,2},{1,3},{2,0},{3,1},{4,6},{5,7},{6,4},{7,5},{8,10},{9,11},{10,... | collective-permute-start | bytes 3538952 | tf_op jit(solution)/shard_map/ppermute | solution.py:897
  149.3 17.0 %collective-permute-start.24 = (bf16[16,192,384]{2,1,0:T(8,128)(2,1)}, bf16[16,192,384]{2,1,0:T(8,128)(2,1)S(1)}, u32[]{:S(2)}, u32[]{:S(2)}) collective-permute-start(bf16[16,192,384]{2,1,0:T(8,128)(2,1)} %get-tuple-element.172), channel_id=1, source_target_pairs={{0,2},{1,3},{2,0},{3,1},{4,6},{5,7},{6,4},{7,5},{8,10},{9,11},{10,... | collective-permute-start | bytes 7077896 | tf_op jit(solution)/shard_map/ppermute | solution.py:957
  150.3 16.5 %copy-start.27 = (bf16[16,192,384]{2,1,0:T(8,128)(2,1)S(1)}, bf16[16,192,384]{2,1,0:T(8,128)(2,1)}, u32[]{:S(2)}) copy-start(bf16[16,192,384]{2,1,0:T(8,128)(2,1)} %get-tuple-element.176) | copy-start | bytes 7077892
  166.2 17.2 %collective-permute-start.26 = (bf16[16,192,384]{2,1,0:T(8,128)(2,1)}, bf16[16,192,384]{2,1,0:T(8,128)(2,1)S(1)}, u32[]{:S(2)}, u32[]{:S(2)}) collective-permute-start(bf16[16,192,384]{2,1,0:T(8,128)(2,1)} %get-tuple-element.180), channel_id=1, source_target_pairs={{0,2},{1,3},{2,0},{3,1},{4,6},{5,7},{6,4},{7,5},{8,10},{9,11},{10,... | collective-permute-start | bytes 7077896 | tf_op jit(solution)/shard_map/ppermute | solution.py:957
  167.2 16.3 %collective-permute-start.25 = (bf16[8,192,384]{2,1,0:T(8,128)(2,1)S(1)}, bf16[8,192,384]{2,1,0:T(8,128)(2,1)S(1)}, u32[]{:S(2)}, u32[]{:S(2)}) collective-permute-start(bf16[8,192,384]{2,1,0:T(8,128)(2,1)S(1)} %add_convert_fusion.3), channel_id=1, source_target_pairs={{0,4},{1,5},{2,3},{3,2},{4,0},{5,1},{6,7},{7,6},{8,12},{9,13},{10,... | collective-permute-start | bytes 3538952 | tf_op jit(solution)/shard_map/ppermute | solution.py:957
  168.0 15.5 %copy-start.25 = (bf16[16,192,384]{2,1,0:T(8,128)(2,1)S(1)}, bf16[16,192,384]{2,1,0:T(8,128)(2,1)}, u32[]{:S(2)}) copy-start(bf16[16,192,384]{2,1,0:T(8,128)(2,1)} %get-tuple-element.177) | copy-start | bytes 7077892
  183.8 21.4 %collective-permute-start.28 = (bf16[8,192,384]{2,1,0:T(8,128)(2,1)S(1)}, bf16[8,192,384]{2,1,0:T(8,128)(2,1)S(1)}, u32[]{:S(2)}, u32[]{:S(2)}) collective-permute-start(bf16[8,192,384]{2,1,0:T(8,128)(2,1)S(1)} %add_convert_fusion.2), channel_id=1, source_target_pairs={{0,4},{1,5},{2,3},{3,2},{4,0},{5,1},{6,7},{7,6},{8,12},{9,13},{10,... | collective-permute-start | bytes 3538952 | tf_op jit(solution)/shard_map/ppermute | solution.py:957
  184.8 16.7 %collective-permute-start.27 = (bf16[4,192,384]{2,1,0:T(8,128)(2,1)S(1)}, bf16[4,192,384]{2,1,0:T(8,128)(2,1)S(1)}, u32[]{:S(2)}, u32[]{:S(2)}) collective-permute-start(bf16[4,192,384]{2,1,0:T(8,128)(2,1)S(1)} %add_convert_fusion.7), channel_id=1, source_target_pairs={{0,1},{1,0},{2,6},{3,7},{4,5},{5,4},{6,2},{7,3},{8,9},{9,8},{10,14... | collective-permute-start | bytes 1769480 | tf_op jit(solution)/shard_map/ppermute | solution.py:957
  205.5 12.6 %collective-permute-start.30 = (bf16[4,192,384]{2,1,0:T(8,128)(2,1)S(1)}, bf16[4,192,384]{2,1,0:T(8,128)(2,1)S(1)}, u32[]{:S(2)}, u32[]{:S(2)}) collective-permute-start(bf16[4,192,384]{2,1,0:T(8,128)(2,1)S(1)} %add_convert_fusion.6), channel_id=1, source_target_pairs={{0,1},{1,0},{2,6},{3,7},{4,5},{5,4},{6,2},{7,3},{8,9},{9,8},{10,14... | collective-permute-start | bytes 1769480 | tf_op jit(solution)/shard_map/ppermute | solution.py:957
  208.1 10.1 %collective-permute-start.29 = (bf16[2,192,384]{2,1,0:T(8,128)(2,1)S(1)}, bf16[2,192,384]{2,1,0:T(8,128)(2,1)S(1)}, u32[]{:S(2)}, u32[]{:S(2)}) collective-permute-start(bf16[2,192,384]{2,1,0:T(8,128)(2,1)S(1)} %add_convert_fusion.11), channel_id=1, source_target_pairs={{0,8},{1,9},{2,10},{3,11},{4,12},{5,13},{6,14},{7,15},{8,0},{9,1},... | collective-permute-start | bytes 884744 | tf_op jit(solution)/shard_map/ppermute | solution.py:957
  218.1 18.2 %copy-start.6 = (bf16[4,192,384]{2,1,0:T(8,128)(2,1)}, bf16[4,192,384]{2,1,0:T(8,128)(2,1)S(1)}, u32[]{:S(2)}) copy-start(bf16[4,192,384]{2,1,0:T(8,128)(2,1)S(1)} %collective-permute-done.30.refs_13_) | copy-start | bytes 1769476
  218.1 16.4 %collective-permute-start.33 = (bf16[16,192,384]{2,1,0:T(8,128)(2,1)}, bf16[16,192,384]{2,1,0:T(8,128)(2,1)S(1)}, u32[]{:S(2)}, u32[]{:S(2)}) collective-permute-start(bf16[16,192,384]{2,1,0:T(8,128)(2,1)} %get-tuple-element.212), channel_id=1, source_target_pairs={{0,2},{1,3},{2,0},{3,1},{4,6},{5,7},{6,4},{7,5},{8,10},{9,11},{10,... | collective-permute-start | bytes 7077896 | tf_op jit(solution)/shard_map/ppermute | solution.py:957
  218.4 16.1 %collective-permute-start.32 = (bf16[2,192,384]{2,1,0:T(8,128)(2,1)S(1)}, bf16[2,192,384]{2,1,0:T(8,128)(2,1)S(1)}, u32[]{:S(2)}, u32[]{:S(2)}) collective-permute-start(bf16[2,192,384]{2,1,0:T(8,128)(2,1)S(1)} %add_convert_fusion.10), channel_id=1, source_target_pairs={{0,8},{1,9},{2,10},{3,11},{4,12},{5,13},{6,14},{7,15},{8,0},{9,1},... | collective-permute-start | bytes 884744 | tf_op jit(solution)/shard_map/ppermute | solution.py:957
  221.0 13.5 %collective-permute-start.31 = (bf16[1,192,384]{2,1,0:T(8,128)(2,1)S(1)}, bf16[1,192,384]{2,1,0:T(8,128)(2,1)S(1)}, u32[]{:S(2)}, u32[]{:S(2)}) collective-permute-start(bf16[1,192,384]{2,1,0:T(8,128)(2,1)S(1)} %add_convert_fusion.15), channel_id=1, source_target_pairs={{0,16},{1,17},{2,18},{3,19},{4,20},{5,21},{6,22},{7,23},{8,24},{9,... | collective-permute-start | bytes 442376 | tf_op jit(solution)/shard_map/ppermute | solution.py:957
  234.5 52.1 %copy-start.4 = (bf16[16,192,384]{2,1,0:T(8,128)(2,1)}, bf16[16,192,384]{2,1,0:T(8,128)(2,1)S(1)}, u32[]{:S(2)}) copy-start(bf16[16,192,384]{2,1,0:T(8,128)(2,1)S(1)} %collective-permute-done.33.refs_15_) | copy-start | bytes 7077892
  234.8 16.3 %collective-permute-start.35 = (bf16[8,192,384]{2,1,0:T(8,128)(2,1)S(1)}, bf16[8,192,384]{2,1,0:T(8,128)(2,1)S(1)}, u32[]{:S(2)}, u32[]{:S(2)}) collective-permute-start(bf16[8,192,384]{2,1,0:T(8,128)(2,1)S(1)} %add_convert_fusion.1), channel_id=1, source_target_pairs={{0,4},{1,5},{2,3},{3,2},{4,0},{5,1},{6,7},{7,6},{8,12},{9,13},{10,... | collective-permute-start | bytes 3538952 | tf_op jit(solution)/shard_map/ppermute | solution.py:957
  237.3 12.9 %collective-permute-start.34 = (bf16[1,192,384]{2,1,0:T(8,128)(2,1)S(1)}, bf16[1,192,384]{2,1,0:T(8,128)(2,1)S(1)}, u32[]{:S(2)}, u32[]{:S(2)}) collective-permute-start(bf16[1,192,384]{2,1,0:T(8,128)(2,1)S(1)} %add_convert_fusion.14), channel_id=1, source_target_pairs={{0,16},{1,17},{2,18},{3,19},{4,20},{5,21},{6,22},{7,23},{8,24},{9,... | collective-permute-start | bytes 442376 | tf_op jit(solution)/shard_map/ppermute | solution.py:957
  251.1 35.5 %copy-start.5 = (bf16[8,192,384]{2,1,0:T(8,128)(2,1)}, bf16[8,192,384]{2,1,0:T(8,128)(2,1)S(1)}, u32[]{:S(2)}) copy-start(bf16[8,192,384]{2,1,0:T(8,128)(2,1)S(1)} %collective-permute-done.35.refs_14_) | copy-start | bytes 3538948
  251.1 4.7 %collective-permute-start.36 = (bf16[16,192,384]{2,1,0:T(8,128)(2,1)}, bf16[16,192,384]{2,1,0:T(8,128)(2,1)S(1)}, u32[]{:S(2)}, u32[]{:S(2)}) collective-permute-start(bf16[16,192,384]{2,1,0:T(8,128)(2,1)} %get-tuple-element.220), channel_id=1, source_target_pairs={{0,2},{1,3},{2,0},{3,1},{4,6},{5,7},{6,4},{7,5},{8,10},{9,11},{10,... | collective-permute-start | bytes 7077896 | tf_op jit(solution)/shard_map/ppermute | solution.py:957
  255.8 29.4 %copy-start.3 = (bf16[16,192,384]{2,1,0:T(8,128)(2,1)}, bf16[16,192,384]{2,1,0:T(8,128)(2,1)S(1)}, u32[]{:S(2)}) copy-start(bf16[16,192,384]{2,1,0:T(8,128)(2,1)S(1)} %collective-permute-done.36.refs_15_) | copy-start | bytes 7077892
  258.3 16.5 %collective-permute-start.37 = (bf16[8,192,384]{2,1,0:T(8,128)(2,1)S(1)}, bf16[8,192,384]{2,1,0:T(8,128)(2,1)S(1)}, u32[]{:S(2)}, u32[]{:S(2)}) collective-permute-start(bf16[8,192,384]{2,1,0:T(8,128)(2,1)S(1)} %add_convert_fusion), channel_id=1, source_target_pairs={{0,4},{1,5},{2,3},{3,2},{4,0},{5,1},{6,7},{7,6},{8,12},{9,13},{10,... | collective-permute-start | bytes 3538952 | tf_op jit(solution)/shard_map/ppermute | solution.py:957
  260.0 14.8 %collective-permute-start.38 = (bf16[4,192,384]{2,1,0:T(8,128)(2,1)S(1)}, bf16[4,192,384]{2,1,0:T(8,128)(2,1)S(1)}, u32[]{:S(2)}, u32[]{:S(2)}) collective-permute-start(bf16[4,192,384]{2,1,0:T(8,128)(2,1)S(1)} %add_convert_fusion.5), channel_id=1, source_target_pairs={{0,8},{1,9},{2,10},{3,11},{4,12},{5,13},{6,14},{7,15},{8,0},{9,1},... | collective-permute-start | bytes 1769480 | tf_op jit(solution)/shard_map/ppermute | solution.py:957
  275.0 10.2 %collective-permute-start.39 = (bf16[4,192,384]{2,1,0:T(8,128)(2,1)S(1)}, bf16[4,192,384]{2,1,0:T(8,128)(2,1)S(1)}, u32[]{:S(2)}, u32[]{:S(2)}) collective-permute-start(bf16[4,192,384]{2,1,0:T(8,128)(2,1)S(1)} %add_convert_fusion.4), channel_id=1, source_target_pairs={{0,1},{1,0},{2,6},{3,7},{4,5},{5,4},{6,2},{7,3},{8,9},{9,8},{10,14... | collective-permute-start | bytes 1769480 | tf_op jit(solution)/shard_map/ppermute | solution.py:957
  276.1 1.3 collective-permute-start.44
  277.4 12.6 %collective-permute-start.45 = (f32[8,768]{1,0:T(8,128)S(1)}, f32[8,768]{1,0:T(8,128)S(1)}, u32[]{:S(2)}, u32[]{:S(2)}) collective-permute-start(f32[8,768]{1,0:T(8,128)S(1)} %add.284), channel_id=1, source_target_pairs={{0,4},{1,5},{2,3},{3,2},{4,0},{5,1},{6,7},{7,6},{8,12},{9,13},{10,... | collective-permute-start | bytes 73736 | tf_op jit(solution)/shard_map/ppermute | solution.py:903
  286.2 13.2 %collective-permute-start.40 = (bf16[2,192,384]{2,1,0:T(8,128)(2,1)}, bf16[2,192,384]{2,1,0:T(8,128)(2,1)}, u32[]{:S(2)}, u32[]{:S(2)}) collective-permute-start(bf16[2,192,384]{2,1,0:T(8,128)(2,1)} %add_convert_fusion.9), channel_id=1, source_target_pairs={{0,8},{1,9},{2,10},{3,11},{4,12},{5,13},{6,14},{7,15},{8,0},{9,1},... | collective-permute-start | bytes 884744 | tf_op jit(solution)/shard_map/ppermute | solution.py:957
  288.4 14.6 %collective-permute-start.42 = (bf16[2,192,384]{2,1,0:T(8,128)(2,1)}, bf16[2,192,384]{2,1,0:T(8,128)(2,1)}, u32[]{:S(2)}, u32[]{:S(2)}) collective-permute-start(bf16[2,192,384]{2,1,0:T(8,128)(2,1)} %add_convert_fusion.8), channel_id=1, source_target_pairs={{0,16},{1,17},{2,18},{3,19},{4,20},{5,21},{6,22},{7,23},{8,24},{9,... | collective-permute-start | bytes 884744 | tf_op jit(solution)/shard_map/ppermute | solution.py:957
  290.6 4.1 %collective-permute-start.46 = (f32[8,768]{1,0:T(8,128)}, f32[8,768]{1,0:T(8,128)}, u32[]{:S(2)}, u32[]{:S(2)}) collective-permute-start(f32[8,768]{1,0:T(8,128)} %add.285), channel_id=1, source_target_pairs={{0,1},{1,0},{2,6},{3,7},{4,5},{5,4},{6,2},{7,3},{8,9},{9,8},{10,14... | collective-permute-start | bytes 73736 | tf_op jit(solution)/shard_map/ppermute | solution.py:906
  295.5 3.8 %collective-permute-start.47 = (f32[8,768]{1,0:T(8,128)S(1)}, f32[8,768]{1,0:T(8,128)S(1)}, u32[]{:S(2)}, u32[]{:S(2)}) collective-permute-start(f32[8,768]{1,0:T(8,128)S(1)} %add.286), channel_id=1, source_target_pairs={{0,8},{1,9},{2,10},{3,11},{4,12},{5,13},{6,14},{7,15},{8,0},{9,1},... | collective-permute-start | bytes 73736 | tf_op jit(solution)/shard_map/ppermute | solution.py:906
  303.0 6.7 %collective-permute-start.48 = (f32[8,768]{1,0:T(8,128)S(1)}, f32[8,768]{1,0:T(8,128)S(1)}, u32[]{:S(2)}, u32[]{:S(2)}) collective-permute-start(f32[8,768]{1,0:T(8,128)S(1)} %add.287), channel_id=1, source_target_pairs={{0,16},{1,17},{2,18},{3,19},{4,20},{5,21},{6,22},{7,23},{8,24},{9,... | collective-permute-start | bytes 73736 | tf_op jit(solution)/shard_map/ppermute | solution.py:908
  305.6 9.2 %collective-permute-start.41 = (bf16[1,192,384]{2,1,0:T(8,128)(2,1)S(1)}, bf16[1,192,384]{2,1,0:T(8,128)(2,1)S(1)}, u32[]{:S(2)}, u32[]{:S(2)}) collective-permute-start(bf16[1,192,384]{2,1,0:T(8,128)(2,1)S(1)} %add_convert_fusion.13), channel_id=1, source_target_pairs={{0,16},{1,17},{2,18},{3,19},{4,20},{5,21},{6,22},{7,23},{8,24},{9,... | collective-permute-start | bytes 442376 | tf_op jit(solution)/shard_map/ppermute | solution.py:957
  308.6 8.9 %collective-permute-start.43 = (bf16[1,192,384]{2,1,0:T(8,128)(2,1)S(1)}, bf16[1,192,384]{2,1,0:T(8,128)(2,1)S(1)}, u32[]{:S(2)}, u32[]{:S(2)}) collective-permute-start(bf16[1,192,384]{2,1,0:T(8,128)(2,1)S(1)} %add_convert_fusion.12), channel_id=1, source_target_pairs={{0,1},{1,0},{2,6},{3,7},{4,5},{5,4},{6,2},{7,3},{8,9},{9,8},{10,14... | collective-permute-start | bytes 442376 | tf_op jit(solution)/shard_map/ppermute | solution.py:957
  (29 other events, 157.2 us)
where the time goes:
time: 324 us; the launch traced here: 320 us
  Pallas kernels  151 us (47%)
  waiting for transfers between devices  73.8 us (23%)
  starting transfers between devices  53.5 us (17%)
  other arithmetic  24.6 us (8%)
  local copies, waits for them, and re-layouts  14.3 us (4%)
    pallas_call x11, Pallas kernels, fused(): pl.pallas_call(kernel, name=name, out_shape=out_shapes, in_specs=[pl.Bloc...  151 us
    ppermute x24, waiting for transfers between devices, go(): return lax.ppermute(v, AXES, perm)  43.3 us
    ppermute x24, starting transfers between devices, go(): return lax.ppermute(v, AXES, perm)  28.8 us
    ppermute x20, waiting for transfers between devices, go(): return lax.ppermute(v.astype(BF16), AXES, perm)  26.2 us
    ppermute x20, starting transfers between devices, go(): return lax.ppermute(v.astype(BF16), AXES, perm)  20.3 us
    convert_element_type x16, other arithmetic, go(): return lax.ppermute(v.astype(BF16), AXES, perm)  13 us
  transfers between devices with their start and end apart: 49, of which 24 were waited for; matrix products, arithmetic and copies ran while one was open for 8% of the time, Pallas kernels for 47%

commit v1 on v0

--- a/solution.py
+++ b/solution.py
@@ -728,6 +728,7 @@
     attend, rest = Loads(), Loads()
     attend.extend(I[:2])
     rest.extend(I[2:])
+    I.later()
     column_attend_back(sm, attend, W, O[:1], G, X[:2])
     ffn_result((), rest, W, O[1:], G, X[2:])
 
@@ -1243,7 +1244,7 @@
     landed = r1.landed() + r2.landed()
     r1.second(sums_two, *landed)
     r2.first(sums_two, *landed)
-    (gq_col, layer_out, mark), _ = run(
+    (gq_col, layer_out, mark, w_col_qkv, w_row_out), _ = run(
         "colt",
         column_back_and_result,
         [ints],
@@ -1253,11 +1254,12 @@
         (),
         [flat, flat, turn],
         landed,
+        ["col_qkv", "row_out"],
     )
     landed = r1.landed() + r2.landed()
     r1.third(mark, *landed)
     r2.second(mark, *landed)
-    (w_col_qkv, w_row_out, after_row_here, grad_after_here), grads = run(
+    (after_row_here, grad_after_here), grads = run(
         "colg",
         product_grads,
         [],
@@ -1267,7 +1269,7 @@
         [3 * width, width],
         (),
         landed,
-        ["col_qkv", "row_out", after_row[1], grad_after],
+        [after_row[1], grad_after],
     )
     r3 = Reduction(plan, grads, ["col_qkv", "col_out"], shards)
     landed = r1.landed() + r2.landed()

time: 324 us -> 319 us (0.985)
  transfers between devices with their start and end apart: 49 -> 49, of which waited for: 24 -> 24; matrix products, arithmetic and copies ran while one was open for 8% -> 8% of each run, Pallas kernels for 47% -> 48%
where the time goes in v1:
time: 319 us; the launch traced here: 315 us
  Pallas kernels  150 us (47%)
  waiting for transfers between devices  74.5 us (23%)
  starting transfers between devices  50.5 us (16%)
  other arithmetic  23.7 us (7%)
  local copies, waits for them, and re-layouts  13.7 us (4%)
    pallas_call x11, Pallas kernels, fused(): pl.pallas_call(kernel, name=name, out_shape=out_shapes, in_specs=[pl.Bloc...  150 us
    ppermute x24, waiting for transfers between devices, go(): return lax.ppermute(v, AXES, perm)  44.1 us
    ppermute x24, starting transfers between devices, go(): return lax.ppermute(v, AXES, perm)  28.8 us
    ppermute x20, waiting for transfers between devices, go(): return lax.ppermute(v.astype(BF16), AXES, perm)  24.1 us
    ppermute x20, starting transfers between devices, go(): return lax.ppermute(v.astype(BF16), AXES, perm)  18.1 us
    convert_element_type x16, other arithmetic, go(): return lax.ppermute(v.astype(BF16), AXES, perm)  12.1 us
  transfers between devices with their start and end apart: 49, of which 24 were waited for; matrix products, arithmetic and copies ran while one was open for 8% of the time, Pallas kernels for 48%

profile of v1, /device:TPU:0, one launch (start us, length us, event | category | flops | bytes accessed | tf_op | source)
XLA Modules:
  0.0 315.1 jit_solution(4833101628851922701)
XLA Ops:
  3.1 4.1 %collective-permute-start = (bf16[1,160,384]{2,1,0:T(8,128)(2,1)S(1)}, bf16[1,160,384]{2,1,0:T(8,128)(2,1)S(1)}, u32[]{:S(2)}, u32[]{:S(2)}) collective-permute-start(bf16[1,160,384]{2,1,0:T(8,128)(2,1)S(1)} %fusion.2), channel_id=1, source_target_pairs={{0,16},{1,17},{2,18},{3,19},{4,20},{5,21},{6,22},{7,23},{8,24},{9,... | collective-permute-start | bytes 368648 | tf_op jit(solution)/shard_map/ppermute | solution.py:898
  7.2 1.5 collective-permute-start.1
  8.7 1.3 fusion.7
  12.2 1.0 collective-permute-done
  13.9 1.0 collective-permute-start.2
  15.0 6.1 %collective-permute-done.2 = bf16[2,160,384]{2,1,0:T(8,128)(2,1)S(1)} collective-permute-done((bf16[2,160,384]{2,1,0:T(8,128)(2,1)S(1)}, bf16[2,160,384]{2,1,0:T(8,128)(2,1)S(1)}, u32[]{:S(2)}, u32[]{:S(2)}) %collective-permute-start.2) | collective-permute-done | bytes 245792 | tf_op jit(solution)/shard_map/ppermute | solution.py:898
  21.2 1.3 collective-permute-start.3
  22.5 3.4 %collective-permute-start.4 = (bf16[1,192,384]{2,1,0:T(8,128)(2,1)S(1)}, bf16[1,192,384]{2,1,0:T(8,128)(2,1)S(1)}, u32[]{:S(2)}, u32[]{:S(2)}) collective-permute-start(bf16[1,192,384]{2,1,0:T(8,128)(2,1)S(1)} %maximum_bitcast_fusion.1), channel_id=1, source_target_pairs={{0,16},{1,17},{2,18},{3,19},{4,20},{5,21},{6,22},{7,23},{8,24},{9,... | collective-permute-start | bytes 442376 | tf_op jit(solution)/shard_map/ppermute | solution.py:898
  25.9 6.4 %collective-permute-done.4 = bf16[1,192,384]{2,1,0:T(8,128)(2,1)S(1)} collective-permute-done((bf16[1,192,384]{2,1,0:T(8,128)(2,1)S(1)}, bf16[1,192,384]{2,1,0:T(8,128)(2,1)S(1)}, u32[]{:S(2)}, u32[]{:S(2)}) %collective-permute-start.4) | collective-permute-done | bytes 147488 | tf_op jit(solution)/shard_map/ppermute | solution.py:898
  33.9 3.4 %collective-permute-start.7 = (bf16[1,240,384]{2,1,0:T(8,128)(2,1)S(1)}, bf16[1,240,384]{2,1,0:T(8,128)(2,1)S(1)}, u32[]{:S(2)}, u32[]{:S(2)}) collective-permute-start(bf16[1,240,384]{2,1,0:T(8,128)(2,1)S(1)} %maximum_bitcast_fusion), channel_id=1, source_target_pairs={{0,16},{1,17},{2,18},{3,19},{4,20},{5,21},{6,22},{7,23},{8,24},{9,... | collective-permute-start | bytes 552968 | tf_op jit(solution)/shard_map/ppermute | solution.py:898
  37.3 7.6 %collective-permute-done.7 = bf16[1,240,384]{2,1,0:T(8,128)(2,1)S(1)} collective-permute-done((bf16[1,240,384]{2,1,0:T(8,128)(2,1)S(1)}, bf16[1,240,384]{2,1,0:T(8,128)(2,1)S(1)}, u32[]{:S(2)}, u32[]{:S(2)}) %collective-permute-start.7) | collective-permute-done | bytes 184352 | tf_op jit(solution)/shard_map/ppermute | solution.py:898
  44.9 1.5 collective-permute-done.6
  47.2 1.6 collective-permute-start.10
  48.8 1.5 collective-permute-start.11
  50.4 8.5 %collective-permute-done.11.refs_11_ = bf16[2,240,384]{2,1,0:T(8,128)(2,1)S(1)} collective-permute-done((bf16[2,240,384]{2,1,0:T(8,128)(2,1)S(1)}, bf16[2,240,384]{2,1,0:T(8,128)(2,1)S(1)}, u32[]{:S(2)}, u32[]{:S(2)}) %collective-permute-start.11) | collective-permute-done | bytes 368672 | tf_op jit(solution)/shard_map/ppermute | solution.py:898
  58.9 1.0 constant_dynamic-update-slice_fusion.12
  60.8 1.6 collective-permute-start.12
  64.7 2.5 collective-permute-start.15
  67.8 11.9 %rowf.1 = (bf16[1024,768]{1,0:T(8,128)(2,1)}, bf16[1024,2304]{1,0:T(8,128)(2,1)}, bf16[1024,768]{1,0:T(8,128)(2,1)S(1)}, bf16[1024,768]{1,0:T(8,128)(2,1)}, f32[...) custom-call(s32[32]{0:T(128)S(1)} %get-tuple-element.230.refs_0_, ...), custom_call_target="tpu_custom_call" | custom-call | flops 9000000 | bytes 27000 | tf_op jit(solution)/shard_map/rowf/pallas_call | solution.py:218
  79.7 1.1 collective-permute-done.15.refs_14_
  80.8 2.8 collective-permute-done.14.refs_13_
  83.6 1.6 collective-permute-done.12.refs_8_.refs_11_.refs_13_
  85.2 3.1 collective-permute-done.16.refs_10_.refs_15_
  88.2 1.6 constant_dynamic-update-slice_fusion.18
  90.2 1.6 collective-permute-start.17
  92.0 1.6 collective-permute-start.19
  93.5 27.9 %colf.1 = (f32[1024,768]{1,0:T(8,128)S(1)}, f32[1024,768]{1,0:T(8,128)}, bf16[1024,768]{1,0:T(8,128)(2,1)}, bf16[1024,2304]{1,0:T(8,128)(2,1)}, bf16[1024,768]{1...) custom-call(s32[32]{0:T(128)S(1)} %get-tuple-element.230.refs_0_, s32[32]{0:T(128)S(1)} %get-tuple-element.231.refs_1_, ...), custom_call_target="tpu_custom_call" | custom-call | flops 8000000 | bytes 24000 | tf_op jit(solution)/shard_map/colf/pallas_call | solution.py:218
  121.6 3.3 %collective-permute-done.20.refs_9_.refs_13_ = bf16[8,240,384]{2,1,0:T(8,128)(2,1)S(1)} collective-permute-done((bf16[8,240,384]{2,1,0:T(8,128)(2,1)S(1)}, bf16[8,240,384]{2,1,0:T(8,128)(2,1)S(1)}, u32[]{:S(2)}, u32[]{:S(2)}) %collective-permute-start.20) | collective-permute-done | bytes 1474592 | tf_op jit(solution)/shard_map/ppermute | solution.py:898
  125.9 14.5 %ffnf.1 = (f32[1024,768]{1,0:T(8,128)}, bf16[1024,768]{1,0:T(8,128)(2,1)}, bf16[1024,3072]{1,0:T(8,128)(2,1)S(1)}, bf16[1024,3072]{1,0:T(8,128)(2,1)}, bf16[1024...) custom-call(s32[32]{0:T(128)S(1)} %get-tuple-element.230.refs_0_, s32[32]{0:T(128)S(1)} %get-tuple-element.231.refs_1_, ...), custom_call_target="tpu_custom_call" | custom-call | flops 12000000 | bytes 36000 | tf_op jit(solution)/shard_map/ffnf/pallas_call | solution.py:218
  140.4 1.0 collective-permute-done.21.refs_6_.refs_7_.refs_9_
  141.4 7.7 %fout.1 = (bf16[1024,768]{1,0:T(8,128)(2,1)S(1)}, bf16[16,192,384]{2,1,0:T(8,128)(2,1)}, bf16[16,192,384]{2,1,0:T(8,128)(2,1)}) custom-call(s32[32]{0:T(128)S(1)} %get-tuple-element.230.refs_0_, s32[32]{0:T(128)S(1)} %get-tuple-element.231.refs_1_, s32[32]{0:T(128)S(1)} %get-tuple-element.232.refs_2_, s32[2]{0:T(128)S(1)} %pad_add_fusion.refs_3_, ...), custom_call_target="tpu_custom_call" | custom-call | flops 7000000 | bytes 21000 | tf_op jit(solution)/shard_map/fout/pallas_call | solution.py:218
  150.2 15.9 %ffnb.1 = (bf16[1024,3072]{1,0:T(8,128)(2,1)S(1)}, bf16[3072,768]{1,0:T(8,128)(2,1)S(1)}, bf16[768,768]{1,0:T(8,128)(2,1)S(1)}, f32[1024,768]{1,0:T(8,128)S(1)},...) custom-call(s32[32]{0:T(128)S(1)} %get-tuple-element.230.refs_0_, s32[32]{0:T(128)S(1)} %get-tuple-element.231.refs_1_, ...), custom_call_target="tpu_custom_call" | custom-call | flops 12000000 | bytes 36000 | tf_op jit(solution)/shard_map/ffnb/pallas_call | solution.py:218
  167.8 12.2 %colb.1 = (f32[1024,768]{1,0:T(8,128)}, bf16[1024,768]{1,0:T(8,128)(2,1)S(1)}, bf16[1024,768]{1,0:T(8,128)(2,1)S(1)}, f32[8,768]{1,0:T(8,128)}, bf16[1024,2304]{...) custom-call(s32[32]{0:T(128)S(1)} %get-tuple-element.230.refs_0_, ...), custom_call_target="tpu_custom_call" | custom-call | flops 10000000 | bytes 30000 | tf_op jit(solution)/shard_map/colb/pallas_call | solution.py:218
  180.0 3.3 %collective-permute-done.25.refs_16_ = bf16[8,192,384]{2,1,0:T(8,128)(2,1)S(1)} collective-permute-done((bf16[8,192,384]{2,1,0:T(8,128)(2,1)S(1)}, bf16[8,192,384]{2,1,0:T(8,128)(2,1)S(1)}, u32[]{:S(2)}, u32[]{:S(2)}) %collective-permute-start.25) | collective-permute-done | bytes 1179680 | tf_op jit(solution)/shard_map/ppermute | solution.py:958
  184.4 1.3 add_convert_fusion.7
  185.7 1.1 collective-permute-start.27
  186.8 16.7 %colt.1 = (bf16[1024,2304]{1,0:T(8,128)(2,1)S(1)}, bf16[1024,768]{1,0:T(8,128)(2,1)}, f32[8,128]{1,0:T(8,128)}, bf16[2304,768]{1,0:T(8,128)(2,1)S(1)}, bf16[768,768]{1,0:T(8,128)(2,1)S(1)}) custom-call(s32[32]{0:T(128)S(1)} %get-tuple-element.230.refs_0_, s32[32]{0:T(128)S(1)} %get-tuple-element.231.refs_1_, s32[32]{0:T(128)S(1)} %get-tuple-element.232.refs_2_, ...), custom_call_target="tpu_custom_call" | custom-call | flops 7000000 | bytes 21000 | tf_op jit(solution)/shard_map/colt/pallas_call | solution.py:218
  203.5 2.7 collective-permute-done.28.refs_10_
  207.2 1.1 add_convert_fusion.11
  208.7 7.4 %colg.1 = (f32[1024,768]{1,0:T(8,128)S(1)}, f32[1024,768]{1,0:T(8,128)S(1)}, bf16[16,192,384]{2,1,0:T(8,128)(2,1)}, bf16[16,192,384]{2,1,0:T(8,128)(2,1)}) custom-call(s32[32]{0:T(128)S(1)} %get-tuple-element.230.refs_0_, s32[32]{0:T(128)S(1)} %get-tuple-element.233.refs_1_, s32[32]{0:T(128)S(1)} %get-tuple-element.232.refs_2_, ...), custom_call_target="tpu_custom_call" | custom-call | flops 7000000 | bytes 21000 | tf_op jit(solution)/shard_map/colg/pallas_call | solution.py:218
  216.5 1.6 collective-permute-start.32
  218.1 1.0 add_convert_fusion.15
  219.2 2.4 collective-permute-start.31
  221.6 11.5 %rowb.1 = (f32[1024,768]{1,0:T(8,128)}, bf16[1024,768]{1,0:T(8,128)(2,1)S(1)}, bf16[1024,768]{1,0:T(8,128)(2,1)S(1)}, f32[8,768]{1,0:T(8,128)}, bf16[1024,2304]{...) custom-call(s32[32]{0:T(128)S(1)} %get-tuple-element.230.refs_0_, ...), custom_call_target="tpu_custom_call" | custom-call | flops 10000000 | bytes 30000 | tf_op jit(solution)/shard_map/rowb/pallas_call | solution.py:218
  235.3 12.4 %rowt.1 = (bf16[1024,2304]{1,0:T(8,128)(2,1)}, bf16[16,192,384]{2,1,0:T(8,128)(2,1)}, bf16[16,192,384]{2,1,0:T(8,128)(2,1)}) custom-call(s32[32]{0:T(128)S(1)} %get-tuple-element.230.refs_0_, s32[32]{0:T(128)S(1)} %get-tuple-element.231.refs_1_, s32[32]{0:T(128)S(1)} %get-tuple-element.232.refs_2_, s32[2]{0:T(128)S(1)} %pad_add_fusion.refs_3_, ...), custom_call_target="tpu_custom_call" | custom-call | flops 13000000 | bytes 39000 | tf_op jit(solution)/shard_map/rowt/pallas_call | solution.py:218
  247.7 2.0 collective-permute-done.35.refs_14_
  249.7 1.9 add_bitcast_fusion.1
  251.6 2.8 collective-permute-done.36.refs_15_
  254.5 2.4 add_convert_fusion
  258.6 11.8 %inpb.1 = (f32[1024,768]{1,0:T(8,128)}, f32[8,768]{1,0:T(8,128)}) custom-call(s32[32]{0:T(128)S(1)} %get-tuple-element.230.refs_0_, s32[32]{0:T(128)S(1)} %get-tuple-element.231.refs_1_, s32[32]{0:T(128)S(1)} %get-tuple-element.232.refs_2_, bf16[1024,2304]{1,0:T(8,128)(2,1)} %get-tuple-element.213.refs_3_, bf16[1024,768]{1,0:T(8,128)(2,1)} %bitcast.48, ...), custom_call_target="tpu_custom_call" | custom-call | flops 9000000 | bytes 27000 | tf_op jit(solution)/shard_map/inpb/pallas_call | solution.py:218
  270.4 2.9 collective-permute-done.38
  273.6 1.1 collective-permute-start.39
  274.8 1.2 collective-permute-done.44
  276.9 7.0 %collective-permute-done.39 = bf16[4,192,384]{2,1,0:T(8,128)(2,1)S(1)} collective-permute-done((bf16[4,192,384]{2,1,0:T(8,128)(2,1)S(1)}, bf16[4,192,384]{2,1,0:T(8,128)(2,1)S(1)}, u32[]{:S(2)}, u32[]{:S(2)}) %collective-permute-start.39) | collective-permute-done | bytes 589856 | tf_op jit(solution)/shard_map/ppermute | solution.py:958
  288.3 3.3 %collective-permute-done.46 = f32[8,768]{1,0:T(8,128)} collective-permute-done((f32[8,768]{1,0:T(8,128)}, f32[8,768]{1,0:T(8,128)}, u32[]{:S(2)}, u32[]{:S(2)}) %collective-permute-start.46) | collective-permute-done | bytes 24608 | tf_op jit(solution)/shard_map/ppermute | solution.py:907
  292.3 1.7 collective-permute-start.47
  294.1 2.0 add_bitcast_fusion
  296.1 1.9 collective-permute-done.47
  298.0 3.1 collective-permute-done.42
  301.0 1.2 add_convert_fusion.12
  302.3 1.3 add_convert_fusion.13
  303.6 3.0 collective-permute-start.41
  309.7 1.3 convert_add_fusion.1
  312.4 1.2 convert_add_fusion
  (188 shorter events, 33.6 us)
Async XLA Ops:
  0.6 21.8 %copy-start.29 = (bf16[384,144]{0,1:T(8,128)(2,1)S(1)}, bf16[384,144]{0,1:T(8,128)(2,1)}, u32[]{:S(2)}) copy-start(bf16[384,144]{0,1:T(8,128)(2,1)} %param.22) | copy-start | bytes 331780
  0.7 21.8 %copy-start.30 = (bf16[48,384]{1,0:T(8,128)(2,1)S(1)}, bf16[48,384]{1,0:T(8,128)(2,1)}, u32[]{:S(2)}) copy-start(bf16[48,384]{1,0:T(8,128)(2,1)} %param.21) | copy-start | bytes 110596
  3.1 10.1 %collective-permute-start = (bf16[1,160,384]{2,1,0:T(8,128)(2,1)S(1)}, bf16[1,160,384]{2,1,0:T(8,128)(2,1)S(1)}, u32[]{:S(2)}, u32[]{:S(2)}) collective-permute-start(bf16[1,160,384]{2,1,0:T(8,128)(2,1)S(1)} %fusion.2), channel_id=1, source_target_pairs={{0,16},{1,17},{2,18},{3,19},{4,20},{5,21},{6,22},{7,23},{8,24},{9,... | collective-permute-start | bytes 368648 | tf_op jit(solution)/shard_map/ppermute | solution.py:898
  7.2 6.0 %collective-permute-start.1 = (bf16[1,192,384]{2,1,0:T(8,128)(2,1)}, bf16[1,192,384]{2,1,0:T(8,128)(2,1)S(1)}, u32[]{:S(2)}, u32[]{:S(2)}) collective-permute-start(bf16[1,192,384]{2,1,0:T(8,128)(2,1)} %bitcast.50), channel_id=1, source_target_pairs={{0,4},{1,5},{2,3},{3,2},{4,0},{5,1},{6,7},{7,6},{8,12},{9,13},{10,... | collective-permute-start | bytes 442376 | tf_op jit(solution)/shard_map/ppermute | solution.py:898
  13.9 7.2 %collective-permute-start.2 = (bf16[2,160,384]{2,1,0:T(8,128)(2,1)S(1)}, bf16[2,160,384]{2,1,0:T(8,128)(2,1)S(1)}, u32[]{:S(2)}, u32[]{:S(2)}) collective-permute-start(bf16[2,160,384]{2,1,0:T(8,128)(2,1)S(1)} %pad_maximum_fusion), channel_id=1, source_target_pairs={{0,8},{1,9},{2,10},{3,11},{4,12},{5,13},{6,14},{7,15},{8,0},{9,1},... | collective-permute-start | bytes 737288 | tf_op jit(solution)/shard_map/ppermute | solution.py:898
  15.0 18.9 %copy-start.28 = (bf16[384,192]{0,1:T(8,128)(2,1)S(1)}, bf16[384,192]{0,1:T(8,128)(2,1)}, u32[]{:S(2)}) copy-start(bf16[384,192]{0,1:T(8,128)(2,1)} %param.24) | copy-start | bytes 442372
  15.0 18.8 %copy-start.31 = (bf16[48,384]{1,0:T(8,128)(2,1)S(1)}, bf16[48,384]{1,0:T(8,128)(2,1)}, u32[]{:S(2)}) copy-start(bf16[48,384]{1,0:T(8,128)(2,1)} %param.23) | copy-start | bytes 110596
  21.2 11.2 %collective-permute-start.3 = (bf16[4,160,384]{2,1,0:T(8,128)(2,1)S(1)}, bf16[4,160,384]{2,1,0:T(8,128)(2,1)S(1)}, u32[]{:S(2)}, u32[]{:S(2)}) collective-permute-start(bf16[4,160,384]{2,1,0:T(8,128)(2,1)S(1)} %constant_dynamic-update-slice_fusion), channel_id=1, source_target_pairs={{0,4},{1,5},{2,3},{3,2},{4,0},{5,1},{6,7},{7,6},{8,12},{9,13},{10,... | collective-permute-start | bytes 1474568 | tf_op jit(solution)/shard_map/ppermute | solution.py:898
  22.5 9.8 %collective-permute-start.4 = (bf16[1,192,384]{2,1,0:T(8,128)(2,1)S(1)}, bf16[1,192,384]{2,1,0:T(8,128)(2,1)S(1)}, u32[]{:S(2)}, u32[]{:S(2)}) collective-permute-start(bf16[1,192,384]{2,1,0:T(8,128)(2,1)S(1)} %maximum_bitcast_fusion.1), channel_id=1, source_target_pairs={{0,16},{1,17},{2,18},{3,19},{4,20},{5,21},{6,22},{7,23},{8,24},{9,... | collective-permute-start | bytes 442376 | tf_op jit(solution)/shard_map/ppermute | solution.py:898
  32.5 26.4 %copy-start.14 = (bf16[8,160,384]{2,1,0:T(8,128)(2,1)}, bf16[8,160,384]{2,1,0:T(8,128)(2,1)S(1)}, u32[]{:S(2)}) copy-start(bf16[8,160,384]{2,1,0:T(8,128)(2,1)S(1)} %constant_dynamic-update-slice_fusion.3.refs_6_.refs_7_) | copy-start | bytes 2949124
  32.5 14.2 %collective-permute-start.5 = (bf16[8,160,384]{2,1,0:T(8,128)(2,1)S(1)}, bf16[8,160,384]{2,1,0:T(8,128)(2,1)S(1)}, u32[]{:S(2)}, u32[]{:S(2)}) collective-permute-start(bf16[8,160,384]{2,1,0:T(8,128)(2,1)S(1)} %constant_dynamic-update-slice_fusion.3.refs_6_.refs_7_), channel_id=1, source_target_pairs={{0,1},{1,0},{2,6},{3,7},{4,5},{5,4},{6,2},{7,3},{8,9},{9,8},{10,14... | collective-permute-start | bytes 2949128 | tf_op jit(solution)/shard_map/ppermute | solution.py:898
  33.1 13.3 %collective-permute-start.6 = (bf16[2,192,384]{2,1,0:T(8,128)(2,1)S(1)}, bf16[2,192,384]{2,1,0:T(8,128)(2,1)S(1)}, u32[]{:S(2)}, u32[]{:S(2)}) collective-permute-start(bf16[2,192,384]{2,1,0:T(8,128)(2,1)S(1)} %constant_dynamic-update-slice_fusion.5), channel_id=1, source_target_pairs={{0,8},{1,9},{2,10},{3,11},{4,12},{5,13},{6,14},{7,15},{8,0},{9,1},... | collective-permute-start | bytes 884744 | tf_op jit(solution)/shard_map/ppermute | solution.py:898
  33.9 11.0 %collective-permute-start.7 = (bf16[1,240,384]{2,1,0:T(8,128)(2,1)S(1)}, bf16[1,240,384]{2,1,0:T(8,128)(2,1)S(1)}, u32[]{:S(2)}, u32[]{:S(2)}) collective-permute-start(bf16[1,240,384]{2,1,0:T(8,128)(2,1)S(1)} %maximum_bitcast_fusion), channel_id=1, source_target_pairs={{0,16},{1,17},{2,18},{3,19},{4,20},{5,21},{6,22},{7,23},{8,24},{9,... | collective-permute-start | bytes 552968 | tf_op jit(solution)/shard_map/ppermute | solution.py:898
  46.6 12.2 %copy-start.18 = (bf16[8,160,384]{2,1,0:T(8,128)(2,1)}, bf16[8,160,384]{2,1,0:T(8,128)(2,1)S(1)}, u32[]{:S(2)}) copy-start(bf16[8,160,384]{2,1,0:T(8,128)(2,1)S(1)} %collective-permute-done.5.refs_7_.refs_8_) | copy-start | bytes 2949124
  46.6 12.2 %collective-permute-start.8 = (bf16[8,160,384]{2,1,0:T(8,128)(2,1)S(1)}, bf16[8,160,384]{2,1,0:T(8,128)(2,1)S(1)}, u32[]{:S(2)}, u32[]{:S(2)}) collective-permute-start(bf16[8,160,384]{2,1,0:T(8,128)(2,1)S(1)} %constant_dynamic-update-slice_fusion.3.refs_6_.refs_7_), channel_id=1, source_target_pairs={{0,2},{1,3},{2,0},{3,1},{4,6},{5,7},{6,4},{7,5},{8,10},{9,11},{10,... | collective-permute-start | bytes 2949128 | tf_op jit(solution)/shard_map/ppermute | solution.py:898
  46.6 12.2 %collective-permute-start.9 = (bf16[8,160,384]{2,1,0:T(8,128)(2,1)S(1)}, bf16[8,160,384]{2,1,0:T(8,128)(2,1)}, u32[]{:S(2)}, u32[]{:S(2)}) collective-permute-start(bf16[8,160,384]{2,1,0:T(8,128)(2,1)S(1)} %collective-permute-done.5.refs_7_.refs_8_), channel_id=1, source_target_pairs={{0,2},{1,3},{2,0},{3,1},{4,6},{5,7},{6,4},{7,5},{8,10},{9,11},{10,... | collective-permute-start | bytes 2949128 | tf_op jit(solution)/shard_map/ppermute | solution.py:898
  47.2 11.6 %collective-permute-start.10 = (bf16[4,192,384]{2,1,0:T(8,128)(2,1)S(1)}, bf16[4,192,384]{2,1,0:T(8,128)(2,1)S(1)}, u32[]{:S(2)}, u32[]{:S(2)}) collective-permute-start(bf16[4,192,384]{2,1,0:T(8,128)(2,1)S(1)} %constant_dynamic-update-slice_fusion.7), channel_id=1, source_target_pairs={{0,4},{1,5},{2,3},{3,2},{4,0},{5,1},{6,7},{7,6},{8,12},{9,13},{10,... | collective-permute-start | bytes 1769480 | tf_op jit(solution)/shard_map/ppermute | solution.py:898
  48.8 10.0 %collective-permute-start.11 = (bf16[2,240,384]{2,1,0:T(8,128)(2,1)S(1)}, bf16[2,240,384]{2,1,0:T(8,128)(2,1)S(1)}, u32[]{:S(2)}, u32[]{:S(2)}) collective-permute-start(bf16[2,240,384]{2,1,0:T(8,128)(2,1)S(1)} %constant_dynamic-update-slice_fusion.9), channel_id=1, source_target_pairs={{0,8},{1,9},{2,10},{3,11},{4,12},{5,13},{6,14},{7,15},{8,0},{9,1},... | collective-permute-start | bytes 1105928 | tf_op jit(solution)/shard_map/ppermute | solution.py:898
  60.7 22.8 %collective-permute-start.13 = (bf16[8,192,384]{2,1,0:T(8,128)(2,1)}, bf16[8,192,384]{2,1,0:T(8,128)(2,1)}, u32[]{:S(2)}, u32[]{:S(2)}) collective-permute-start(bf16[8,192,384]{2,1,0:T(8,128)(2,1)} %constant_dynamic-update-slice_fusion.11.refs_7_.refs_12_), channel_id=1, source_target_pairs={{0,2},{1,3},{2,0},{3,1},{4,6},{5,7},{6,4},{7,5},{8,10},{9,11},{10,... | collective-permute-start | bytes 3538952 | tf_op jit(solution)/shard_map/ppermute | solution.py:898
  60.8 24.4 %collective-permute-start.12 = (bf16[8,192,384]{2,1,0:T(8,128)(2,1)}, bf16[8,192,384]{2,1,0:T(8,128)(2,1)}, u32[]{:S(2)}, u32[]{:S(2)}) collective-permute-start(bf16[8,192,384]{2,1,0:T(8,128)(2,1)} %constant_dynamic-update-slice_fusion.11.refs_7_.refs_12_), channel_id=1, source_target_pairs={{0,1},{1,0},{2,6},{3,7},{4,5},{5,4},{6,2},{7,3},{8,9},{9,8},{10,14... | collective-permute-start | bytes 3538952 | tf_op jit(solution)/shard_map/ppermute | solution.py:898
  64.0 19.6 %collective-permute-start.14 = (bf16[4,240,384]{2,1,0:T(8,128)(2,1)}, bf16[4,240,384]{2,1,0:T(8,128)(2,1)S(1)}, u32[]{:S(2)}, u32[]{:S(2)}) collective-permute-start(bf16[4,240,384]{2,1,0:T(8,128)(2,1)} %constant_dynamic-update-slice_fusion.13), channel_id=1, source_target_pairs={{0,4},{1,5},{2,3},{3,2},{4,0},{5,1},{6,7},{7,6},{8,12},{9,13},{10,... | collective-permute-start | bytes 2211848 | tf_op jit(solution)/shard_map/ppermute | solution.py:898
  64.7 16.1 %collective-permute-start.15 = (bf16[2,192,384]{2,1,0:T(8,128)(2,1)S(1)}, bf16[2,192,384]{2,1,0:T(8,128)(2,1)S(1)}, u32[]{:S(2)}, u32[]{:S(2)}) collective-permute-start(bf16[2,192,384]{2,1,0:T(8,128)(2,1)S(1)} %constant_dynamic-update-slice_fusion.15), channel_id=1, source_target_pairs={{0,16},{1,17},{2,18},{3,19},{4,20},{5,21},{6,22},{7,23},{8,24},{9,... | collective-permute-start | bytes 884744 | tf_op jit(solution)/shard_map/ppermute | solution.py:898
  85.2 3.1 collective-permute-start.16
  90.0 31.5 %copy-start.11 = (bf16[8,240,384]{2,1,0:T(8,128)(2,1)}, bf16[8,240,384]{2,1,0:T(8,128)(2,1)S(1)}, u32[]{:S(2)}) copy-start(bf16[8,240,384]{2,1,0:T(8,128)(2,1)S(1)} %constant_dynamic-update-slice_fusion.17.refs_6_.refs_10_) | copy-start | bytes 4423684
  90.0 31.5 %collective-permute-start.18 = (bf16[8,240,384]{2,1,0:T(8,128)(2,1)S(1)}, bf16[8,240,384]{2,1,0:T(8,128)(2,1)S(1)}, u32[]{:S(2)}, u32[]{:S(2)}) collective-permute-start(bf16[8,240,384]{2,1,0:T(8,128)(2,1)S(1)} %constant_dynamic-update-slice_fusion.17.refs_6_.refs_10_), channel_id=1, source_target_pairs={{0,2},{1,3},{2,0},{3,1},{4,6},{5,7},{6,4},{7,5},{8,10},{9,11},{10,... | collective-permute-start | bytes 4423688 | tf_op jit(solution)/shard_map/ppermute | solution.py:898
  90.2 31.3 %collective-permute-start.17 = (bf16[8,240,384]{2,1,0:T(8,128)(2,1)S(1)}, bf16[8,240,384]{2,1,0:T(8,128)(2,1)S(1)}, u32[]{:S(2)}, u32[]{:S(2)}) collective-permute-start(bf16[8,240,384]{2,1,0:T(8,128)(2,1)S(1)} %constant_dynamic-update-slice_fusion.17.refs_6_.refs_10_), channel_id=1, source_target_pairs={{0,1},{1,0},{2,6},{3,7},{4,5},{5,4},{6,2},{7,3},{8,9},{9,8},{10,14... | collective-permute-start | bytes 4423688 | tf_op jit(solution)/shard_map/ppermute | solution.py:898
  92.0 29.5 %collective-permute-start.19 = (bf16[4,192,384]{2,1,0:T(8,128)(2,1)S(1)}, bf16[4,192,384]{2,1,0:T(8,128)(2,1)S(1)}, u32[]{:S(2)}, u32[]{:S(2)}) collective-permute-start(bf16[4,192,384]{2,1,0:T(8,128)(2,1)S(1)} %constant_dynamic-update-slice_fusion.19), channel_id=1, source_target_pairs={{0,8},{1,9},{2,10},{3,11},{4,12},{5,13},{6,14},{7,15},{8,0},{9,1},... | collective-permute-start | bytes 1769480 | tf_op jit(solution)/shard_map/ppermute | solution.py:898
  121.5 3.3 %collective-permute-start.20 = (bf16[8,240,384]{2,1,0:T(8,128)(2,1)S(1)}, bf16[8,240,384]{2,1,0:T(8,128)(2,1)S(1)}, u32[]{:S(2)}, u32[]{:S(2)}) collective-permute-start(bf16[8,240,384]{2,1,0:T(8,128)(2,1)S(1)} %collective-permute-done.17.refs_7_.refs_11_), channel_id=1, source_target_pairs={{0,2},{1,3},{2,0},{3,1},{4,6},{5,7},{6,4},{7,5},{8,10},{9,11},{10,... | collective-permute-start | bytes 4423688 | tf_op jit(solution)/shard_map/ppermute | solution.py:898
  125.0 15.4 %copy-start.13 = (bf16[8,192,384]{2,1,0:T(8,128)(2,1)}, bf16[8,192,384]{2,1,0:T(8,128)(2,1)S(1)}, u32[]{:S(2)}) copy-start(bf16[8,192,384]{2,1,0:T(8,128)(2,1)S(1)} %constant_dynamic-update-slice_fusion.21.refs_6_.refs_8_) | copy-start | bytes 3538948
  125.0 15.4 %collective-permute-start.22 = (bf16[8,192,384]{2,1,0:T(8,128)(2,1)S(1)}, bf16[8,192,384]{2,1,0:T(8,128)(2,1)S(1)}, u32[]{:S(2)}, u32[]{:S(2)}) collective-permute-start(bf16[8,192,384]{2,1,0:T(8,128)(2,1)S(1)} %constant_dynamic-update-slice_fusion.21.refs_6_.refs_8_), channel_id=1, source_target_pairs={{0,2},{1,3},{2,0},{3,1},{4,6},{5,7},{6,4},{7,5},{8,10},{9,11},{10,... | collective-permute-start | bytes 3538952 | tf_op jit(solution)/shard_map/ppermute | solution.py:898
  125.2 16.2 %collective-permute-start.21 = (bf16[8,192,384]{2,1,0:T(8,128)(2,1)S(1)}, bf16[8,192,384]{2,1,0:T(8,128)(2,1)S(1)}, u32[]{:S(2)}, u32[]{:S(2)}) collective-permute-start(bf16[8,192,384]{2,1,0:T(8,128)(2,1)S(1)} %constant_dynamic-update-slice_fusion.21.refs_6_.refs_8_), channel_id=1, source_target_pairs={{0,1},{1,0},{2,6},{3,7},{4,5},{5,4},{6,2},{7,3},{8,9},{9,8},{10,14... | collective-permute-start | bytes 3538952 | tf_op jit(solution)/shard_map/ppermute | solution.py:898
  141.4 7.8 %collective-permute-start.23 = (bf16[8,192,384]{2,1,0:T(8,128)(2,1)S(1)}, bf16[8,192,384]{2,1,0:T(8,128)(2,1)S(1)}, u32[]{:S(2)}, u32[]{:S(2)}) collective-permute-start(bf16[8,192,384]{2,1,0:T(8,128)(2,1)S(1)} %collective-permute-done.21.refs_6_.refs_7_.refs_9_), channel_id=1, source_target_pairs={{0,2},{1,3},{2,0},{3,1},{4,6},{5,7},{6,4},{7,5},{8,10},{9,11},{10,... | collective-permute-start | bytes 3538952 | tf_op jit(solution)/shard_map/ppermute | solution.py:898
  149.2 16.9 %collective-permute-start.24 = (bf16[16,192,384]{2,1,0:T(8,128)(2,1)}, bf16[16,192,384]{2,1,0:T(8,128)(2,1)S(1)}, u32[]{:S(2)}, u32[]{:S(2)}) collective-permute-start(bf16[16,192,384]{2,1,0:T(8,128)(2,1)} %get-tuple-element.172), channel_id=1, source_target_pairs={{0,2},{1,3},{2,0},{3,1},{4,6},{5,7},{6,4},{7,5},{8,10},{9,11},{10,... | collective-permute-start | bytes 7077896 | tf_op jit(solution)/shard_map/ppermute | solution.py:958
  150.2 16.5 %copy-start.21 = (bf16[16,192,384]{2,1,0:T(8,128)(2,1)S(1)}, bf16[16,192,384]{2,1,0:T(8,128)(2,1)}, u32[]{:S(2)}) copy-start(bf16[16,192,384]{2,1,0:T(8,128)(2,1)} %get-tuple-element.176) | copy-start | bytes 7077892
  166.2 17.2 %collective-permute-start.26 = (bf16[16,192,384]{2,1,0:T(8,128)(2,1)}, bf16[16,192,384]{2,1,0:T(8,128)(2,1)S(1)}, u32[]{:S(2)}, u32[]{:S(2)}) collective-permute-start(bf16[16,192,384]{2,1,0:T(8,128)(2,1)} %get-tuple-element.180), channel_id=1, source_target_pairs={{0,2},{1,3},{2,0},{3,1},{4,6},{5,7},{6,4},{7,5},{8,10},{9,11},{10,... | collective-permute-start | bytes 7077896 | tf_op jit(solution)/shard_map/ppermute | solution.py:958
  167.1 16.3 %collective-permute-start.25 = (bf16[8,192,384]{2,1,0:T(8,128)(2,1)S(1)}, bf16[8,192,384]{2,1,0:T(8,128)(2,1)S(1)}, u32[]{:S(2)}, u32[]{:S(2)}) collective-permute-start(bf16[8,192,384]{2,1,0:T(8,128)(2,1)S(1)} %add_convert_fusion.3), channel_id=1, source_target_pairs={{0,4},{1,5},{2,3},{3,2},{4,0},{5,1},{6,7},{7,6},{8,12},{9,13},{10,... | collective-permute-start | bytes 3538952 | tf_op jit(solution)/shard_map/ppermute | solution.py:958
  167.8 15.5 %copy-start.19 = (bf16[16,192,384]{2,1,0:T(8,128)(2,1)S(1)}, bf16[16,192,384]{2,1,0:T(8,128)(2,1)}, u32[]{:S(2)}) copy-start(bf16[16,192,384]{2,1,0:T(8,128)(2,1)} %get-tuple-element.177) | copy-start | bytes 7077892
  183.7 22.5 %collective-permute-start.28 = (bf16[8,192,384]{2,1,0:T(8,128)(2,1)S(1)}, bf16[8,192,384]{2,1,0:T(8,128)(2,1)S(1)}, u32[]{:S(2)}, u32[]{:S(2)}) collective-permute-start(bf16[8,192,384]{2,1,0:T(8,128)(2,1)S(1)} %add_convert_fusion.2), channel_id=1, source_target_pairs={{0,4},{1,5},{2,3},{3,2},{4,0},{5,1},{6,7},{7,6},{8,12},{9,13},{10,... | collective-permute-start | bytes 3538952 | tf_op jit(solution)/shard_map/ppermute | solution.py:958
  185.7 17.8 %collective-permute-start.27 = (bf16[4,192,384]{2,1,0:T(8,128)(2,1)S(1)}, bf16[4,192,384]{2,1,0:T(8,128)(2,1)S(1)}, u32[]{:S(2)}, u32[]{:S(2)}) collective-permute-start(bf16[4,192,384]{2,1,0:T(8,128)(2,1)S(1)} %add_convert_fusion.7), channel_id=1, source_target_pairs={{0,1},{1,0},{2,6},{3,7},{4,5},{5,4},{6,2},{7,3},{8,9},{9,8},{10,14... | collective-permute-start | bytes 1769480 | tf_op jit(solution)/shard_map/ppermute | solution.py:958
  206.2 28.1 %copy-start.5 = (bf16[8,192,384]{2,1,0:T(8,128)(2,1)}, bf16[8,192,384]{2,1,0:T(8,128)(2,1)S(1)}, u32[]{:S(2)}) copy-start(bf16[8,192,384]{2,1,0:T(8,128)(2,1)S(1)} %collective-permute-done.28.refs_10_) | copy-start | bytes 3538948
  206.4 9.9 %collective-permute-start.30 = (bf16[4,192,384]{2,1,0:T(8,128)(2,1)S(1)}, bf16[4,192,384]{2,1,0:T(8,128)(2,1)S(1)}, u32[]{:S(2)}, u32[]{:S(2)}) collective-permute-start(bf16[4,192,384]{2,1,0:T(8,128)(2,1)S(1)} %add_convert_fusion.6), channel_id=1, source_target_pairs={{0,1},{1,0},{2,6},{3,7},{4,5},{5,4},{6,2},{7,3},{8,9},{9,8},{10,14... | collective-permute-start | bytes 1769480 | tf_op jit(solution)/shard_map/ppermute | solution.py:958
  208.3 7.8 %collective-permute-start.29 = (bf16[2,192,384]{2,1,0:T(8,128)(2,1)S(1)}, bf16[2,192,384]{2,1,0:T(8,128)(2,1)S(1)}, u32[]{:S(2)}, u32[]{:S(2)}) collective-permute-start(bf16[2,192,384]{2,1,0:T(8,128)(2,1)S(1)} %add_convert_fusion.11), channel_id=1, source_target_pairs={{0,8},{1,9},{2,10},{3,11},{4,12},{5,13},{6,14},{7,15},{8,0},{9,1},... | collective-permute-start | bytes 884744 | tf_op jit(solution)/shard_map/ppermute | solution.py:958
  216.3 18.0 %copy-start.6 = (bf16[4,192,384]{2,1,0:T(8,128)(2,1)}, bf16[4,192,384]{2,1,0:T(8,128)(2,1)S(1)}, u32[]{:S(2)}) copy-start(bf16[4,192,384]{2,1,0:T(8,128)(2,1)S(1)} %collective-permute-done.30.refs_13_) | copy-start | bytes 1769476
  216.3 16.8 %collective-permute-start.33 = (bf16[16,192,384]{2,1,0:T(8,128)(2,1)}, bf16[16,192,384]{2,1,0:T(8,128)(2,1)S(1)}, u32[]{:S(2)}, u32[]{:S(2)}) collective-permute-start(bf16[16,192,384]{2,1,0:T(8,128)(2,1)} %get-tuple-element.212), channel_id=1, source_target_pairs={{0,2},{1,3},{2,0},{3,1},{4,6},{5,7},{6,4},{7,5},{8,10},{9,11},{10,... | collective-permute-start | bytes 7077896 | tf_op jit(solution)/shard_map/ppermute | solution.py:958
  216.5 16.6 %collective-permute-start.32 = (bf16[2,192,384]{2,1,0:T(8,128)(2,1)S(1)}, bf16[2,192,384]{2,1,0:T(8,128)(2,1)S(1)}, u32[]{:S(2)}, u32[]{:S(2)}) collective-permute-start(bf16[2,192,384]{2,1,0:T(8,128)(2,1)S(1)} %add_convert_fusion.10), channel_id=1, source_target_pairs={{0,8},{1,9},{2,10},{3,11},{4,12},{5,13},{6,14},{7,15},{8,0},{9,1},... | collective-permute-start | bytes 884744 | tf_op jit(solution)/shard_map/ppermute | solution.py:958
  219.2 13.9 %collective-permute-start.31 = (bf16[1,192,384]{2,1,0:T(8,128)(2,1)S(1)}, bf16[1,192,384]{2,1,0:T(8,128)(2,1)S(1)}, u32[]{:S(2)}, u32[]{:S(2)}) collective-permute-start(bf16[1,192,384]{2,1,0:T(8,128)(2,1)S(1)} %add_convert_fusion.15), channel_id=1, source_target_pairs={{0,16},{1,17},{2,18},{3,19},{4,20},{5,21},{6,22},{7,23},{8,24},{9,... | collective-permute-start | bytes 442376 | tf_op jit(solution)/shard_map/ppermute | solution.py:958
  233.1 51.9 %copy-start.4 = (bf16[16,192,384]{2,1,0:T(8,128)(2,1)}, bf16[16,192,384]{2,1,0:T(8,128)(2,1)S(1)}, u32[]{:S(2)}) copy-start(bf16[16,192,384]{2,1,0:T(8,128)(2,1)S(1)} %collective-permute-done.33.refs_15_) | copy-start | bytes 7077892
  233.4 16.3 %collective-permute-start.35 = (bf16[8,192,384]{2,1,0:T(8,128)(2,1)S(1)}, bf16[8,192,384]{2,1,0:T(8,128)(2,1)S(1)}, u32[]{:S(2)}, u32[]{:S(2)}) collective-permute-start(bf16[8,192,384]{2,1,0:T(8,128)(2,1)S(1)} %add_convert_fusion.1), channel_id=1, source_target_pairs={{0,4},{1,5},{2,3},{3,2},{4,0},{5,1},{6,7},{7,6},{8,12},{9,13},{10,... | collective-permute-start | bytes 3538952 | tf_op jit(solution)/shard_map/ppermute | solution.py:958
  234.4 13.3 %collective-permute-start.34 = (bf16[1,192,384]{2,1,0:T(8,128)(2,1)S(1)}, bf16[1,192,384]{2,1,0:T(8,128)(2,1)S(1)}, u32[]{:S(2)}, u32[]{:S(2)}) collective-permute-start(bf16[1,192,384]{2,1,0:T(8,128)(2,1)S(1)} %add_convert_fusion.14), channel_id=1, source_target_pairs={{0,16},{1,17},{2,18},{3,19},{4,20},{5,21},{6,22},{7,23},{8,24},{9,... | collective-permute-start | bytes 442376 | tf_op jit(solution)/shard_map/ppermute | solution.py:958
  249.7 4.7 %collective-permute-start.36 = (bf16[16,192,384]{2,1,0:T(8,128)(2,1)}, bf16[16,192,384]{2,1,0:T(8,128)(2,1)S(1)}, u32[]{:S(2)}, u32[]{:S(2)}) collective-permute-start(bf16[16,192,384]{2,1,0:T(8,128)(2,1)} %get-tuple-element.220), channel_id=1, source_target_pairs={{0,2},{1,3},{2,0},{3,1},{4,6},{5,7},{6,4},{7,5},{8,10},{9,11},{10,... | collective-permute-start | bytes 7077896 | tf_op jit(solution)/shard_map/ppermute | solution.py:958
  254.5 29.4 %copy-start.3 = (bf16[16,192,384]{2,1,0:T(8,128)(2,1)}, bf16[16,192,384]{2,1,0:T(8,128)(2,1)S(1)}, u32[]{:S(2)}) copy-start(bf16[16,192,384]{2,1,0:T(8,128)(2,1)S(1)} %collective-permute-done.36.refs_15_) | copy-start | bytes 7077892
  256.9 16.5 %collective-permute-start.37 = (bf16[8,192,384]{2,1,0:T(8,128)(2,1)S(1)}, bf16[8,192,384]{2,1,0:T(8,128)(2,1)S(1)}, u32[]{:S(2)}, u32[]{:S(2)}) collective-permute-start(bf16[8,192,384]{2,1,0:T(8,128)(2,1)S(1)} %add_convert_fusion), channel_id=1, source_target_pairs={{0,4},{1,5},{2,3},{3,2},{4,0},{5,1},{6,7},{7,6},{8,12},{9,13},{10,... | collective-permute-start | bytes 3538952 | tf_op jit(solution)/shard_map/ppermute | solution.py:958
  258.0 15.4 %collective-permute-start.38 = (bf16[4,192,384]{2,1,0:T(8,128)(2,1)S(1)}, bf16[4,192,384]{2,1,0:T(8,128)(2,1)S(1)}, u32[]{:S(2)}, u32[]{:S(2)}) collective-permute-start(bf16[4,192,384]{2,1,0:T(8,128)(2,1)S(1)} %add_convert_fusion.5), channel_id=1, source_target_pairs={{0,8},{1,9},{2,10},{3,11},{4,12},{5,13},{6,14},{7,15},{8,0},{9,1},... | collective-permute-start | bytes 1769480 | tf_op jit(solution)/shard_map/ppermute | solution.py:958
  273.4 11.7 %copy-start.23 = (bf16[4,192,384]{2,1,0:T(8,128)(2,1)}, bf16[4,192,384]{2,1,0:T(8,128)(2,1)S(1)}, u32[]{:S(2)}) copy-start(bf16[4,192,384]{2,1,0:T(8,128)(2,1)S(1)} %collective-permute-done.38) | copy-start | bytes 1769476
  273.6 10.2 %collective-permute-start.39 = (bf16[4,192,384]{2,1,0:T(8,128)(2,1)S(1)}, bf16[4,192,384]{2,1,0:T(8,128)(2,1)S(1)}, u32[]{:S(2)}, u32[]{:S(2)}) collective-permute-start(bf16[4,192,384]{2,1,0:T(8,128)(2,1)S(1)} %add_convert_fusion.4), channel_id=1, source_target_pairs={{0,1},{1,0},{2,6},{3,7},{4,5},{5,4},{6,2},{7,3},{8,9},{9,8},{10,14... | collective-permute-start | bytes 1769480 | tf_op jit(solution)/shard_map/ppermute | solution.py:958
  274.7 1.3 collective-permute-start.44
  276.0 10.8 %collective-permute-start.45 = (f32[8,768]{1,0:T(8,128)S(1)}, f32[8,768]{1,0:T(8,128)S(1)}, u32[]{:S(2)}, u32[]{:S(2)}) collective-permute-start(f32[8,768]{1,0:T(8,128)S(1)} %add.284), channel_id=1, source_target_pairs={{0,4},{1,5},{2,3},{3,2},{4,0},{5,1},{6,7},{7,6},{8,12},{9,13},{10,... | collective-permute-start | bytes 73736 | tf_op jit(solution)/shard_map/ppermute | solution.py:904
  284.7 13.2 %collective-permute-start.40 = (bf16[2,192,384]{2,1,0:T(8,128)(2,1)}, bf16[2,192,384]{2,1,0:T(8,128)(2,1)}, u32[]{:S(2)}, u32[]{:S(2)}) collective-permute-start(bf16[2,192,384]{2,1,0:T(8,128)(2,1)} %add_convert_fusion.9), channel_id=1, source_target_pairs={{0,8},{1,9},{2,10},{3,11},{4,12},{5,13},{6,14},{7,15},{8,0},{9,1},... | collective-permute-start | bytes 884744 | tf_op jit(solution)/shard_map/ppermute | solution.py:958
  285.9 15.1 %collective-permute-start.42 = (bf16[2,192,384]{2,1,0:T(8,128)(2,1)}, bf16[2,192,384]{2,1,0:T(8,128)(2,1)}, u32[]{:S(2)}, u32[]{:S(2)}) collective-permute-start(bf16[2,192,384]{2,1,0:T(8,128)(2,1)} %add_convert_fusion.8), channel_id=1, source_target_pairs={{0,16},{1,17},{2,18},{3,19},{4,20},{5,21},{6,22},{7,23},{8,24},{9,... | collective-permute-start | bytes 884744 | tf_op jit(solution)/shard_map/ppermute | solution.py:958
  287.4 4.1 %collective-permute-start.46 = (f32[8,768]{1,0:T(8,128)}, f32[8,768]{1,0:T(8,128)}, u32[]{:S(2)}, u32[]{:S(2)}) collective-permute-start(f32[8,768]{1,0:T(8,128)} %add.285), channel_id=1, source_target_pairs={{0,1},{1,0},{2,6},{3,7},{4,5},{5,4},{6,2},{7,3},{8,9},{9,8},{10,14... | collective-permute-start | bytes 73736 | tf_op jit(solution)/shard_map/ppermute | solution.py:907
  292.3 5.6 %collective-permute-start.47 = (f32[8,768]{1,0:T(8,128)S(1)}, f32[8,768]{1,0:T(8,128)S(1)}, u32[]{:S(2)}, u32[]{:S(2)}) collective-permute-start(f32[8,768]{1,0:T(8,128)S(1)} %add.286), channel_id=1, source_target_pairs={{0,8},{1,9},{2,10},{3,11},{4,12},{5,13},{6,14},{7,15},{8,0},{9,1},... | collective-permute-start | bytes 73736 | tf_op jit(solution)/shard_map/ppermute | solution.py:907
  301.0 6.4 %collective-permute-start.48 = (f32[8,768]{1,0:T(8,128)S(1)}, f32[8,768]{1,0:T(8,128)S(1)}, u32[]{:S(2)}, u32[]{:S(2)}) collective-permute-start(f32[8,768]{1,0:T(8,128)S(1)} %add.287), channel_id=1, source_target_pairs={{0,16},{1,17},{2,18},{3,19},{4,20},{5,21},{6,22},{7,23},{8,24},{9,... | collective-permute-start | bytes 73736 | tf_op jit(solution)/shard_map/ppermute | solution.py:909
  303.6 6.1 %collective-permute-start.41 = (bf16[1,192,384]{2,1,0:T(8,128)(2,1)S(1)}, bf16[1,192,384]{2,1,0:T(8,128)(2,1)S(1)}, u32[]{:S(2)}, u32[]{:S(2)}) collective-permute-start(bf16[1,192,384]{2,1,0:T(8,128)(2,1)S(1)} %add_convert_fusion.13), channel_id=1, source_target_pairs={{0,16},{1,17},{2,18},{3,19},{4,20},{5,21},{6,22},{7,23},{8,24},{9,... | collective-permute-start | bytes 442376 | tf_op jit(solution)/shard_map/ppermute | solution.py:958
  306.6 5.8 %collective-permute-start.43 = (bf16[1,192,384]{2,1,0:T(8,128)(2,1)S(1)}, bf16[1,192,384]{2,1,0:T(8,128)(2,1)S(1)}, u32[]{:S(2)}, u32[]{:S(2)}) collective-permute-start(bf16[1,192,384]{2,1,0:T(8,128)(2,1)S(1)} %add_convert_fusion.12), channel_id=1, source_target_pairs={{0,1},{1,0},{2,6},{3,7},{4,5},{5,4},{6,2},{7,3},{8,9},{9,8},{10,14... | collective-permute-start | bytes 442376 | tf_op jit(solution)/shard_map/ppermute | solution.py:958
  (21 other events, 103.4 us)
